TPU v7x, 32 devices: a whole 2x2x4 slice. The times are simulated.
32 devices in a mesh: level: 4 (over x, core), space: 8 (over z, y).
Axes of the slice: x: 2, y: 2, z: 4, core: 2. Of those that a mesh axis runs over, the one named last changes fastest.
Arguments:
- fc_long: bfloat16 [704, 4, 8, 3, 1440], P('space', 'level'), may hold values from -6 to 6
- fc_short: bfloat16 [704, 4, 8, 3, 1440], P('space', 'level'), may hold values from -6 to 6
Outputs:
- cross: float32 [2, 3, 4, 4, 448, 384], P(None, None, 'level', None, 'space')
All inputs are finite; a program needn't handle non-finite values.
Results may differ from a plain program's by a relative error of at most 0.0077.
Values may be sent and summed in bfloat16 or wider, within the bound.
A program may use at most 64 MiB of HBM per device.

v0:
```python
import math

import jax
import jax.numpy as jnp
from jax import lax
from jax.sharding import PartitionSpec as P

LAT = 704
MK = 448
NL = 384


def from_behind(block, axis, distance):
    devices = range(lax.axis_size(axis))
    route = [((i - distance) % len(devices), i) for i in devices]
    return lax.ppermute(block, axis, route)


def zonal_table(lon_size, wave_total, space_size):
    wave_local = wave_total // space_size
    lon_index = jnp.arange(lon_size, dtype=jnp.int32)[:, None, None]
    wave_index = (
        jnp.arange(space_size, dtype=jnp.int32)[:, None] * wave_local
        + jnp.arange(wave_local, dtype=jnp.int32)[None, :]
    )[None]
    phase_int = lon_index * wave_index % lon_size
    angle_rad = 2.0 * math.pi / lon_size * phase_int.astype(jnp.float32)
    table = jnp.stack([jnp.cos(angle_rad), -jnp.sin(angle_rad)], axis=2) / math.sqrt(lon_size)
    return table.astype(jnp.bfloat16)


def merid_table(lat_size, wave_total):
    lat_index = jnp.arange(lat_size, dtype=jnp.int32)[:, None]
    wave_index = jnp.arange(wave_total, dtype=jnp.int32)[None, :] - wave_total // 2
    phase_int = lat_index * wave_index % lat_size
    angle_rad = 2.0 * math.pi / lat_size * phase_int.astype(jnp.float32)
    table = jnp.stack([jnp.cos(angle_rad), jnp.sin(angle_rad)], axis=1) / math.sqrt(lat_size)
    return table.astype(jnp.bfloat16)


def cross_pair(own_spec, other_spec):
    own_spec = own_spec.astype(jnp.float32)
    other_spec = other_spec.astype(jnp.float32)
    pattern = "savkl,sbvkl->vabkl"
    highest = lax.Precision.HIGHEST
    co_spec = jnp.einsum(pattern, own_spec[0], other_spec[0], precision=highest) + jnp.einsum(
        pattern, own_spec[1], other_spec[1], precision=highest
    )
    quad_spec = jnp.einsum(pattern, own_spec[1], other_spec[0], precision=highest) - jnp.einsum(
        pattern, own_spec[0], other_spec[1], precision=highest
    )
    return jnp.stack([co_spec, quad_spec]) / own_spec.shape[1]


def mirror(pair_result):
    return jnp.stack([jnp.swapaxes(pair_result[0], 1, 2), -jnp.swapaxes(pair_result[1], 1, 2)])


def on_device(fc_long, fc_short):
    lat_local, lev_local, sample_count, var_count, lon_size = fc_long.shape
    space_size = lax.axis_size("space")
    wave_local = MK // space_size
    diff_field = (fc_long.astype(jnp.float32) - fc_short.astype(jnp.float32)).astype(jnp.bfloat16)
    zonal_tab = zonal_table(lon_size, MK, space_size)
    merid_tab = merid_table(LAT, NL)
    zonal_coeff = jnp.einsum(
        "yasvx,xpuk->ypsavuk", diff_field, zonal_tab, preferred_element_type=jnp.float32
    ).astype(jnp.bfloat16)
    zonal_coeff = zonal_coeff.reshape(
        lat_local, space_size, sample_count, lev_local * var_count * 2 * wave_local
    )
    columns = lax.all_to_all(zonal_coeff, "space", split_axis=1, concat_axis=0, tiled=True)
    total_lat, unused_one, item_count, row_width = columns.shape
    columns = columns.reshape(total_lat, item_count, lev_local, var_count, 2, wave_local)
    products = jnp.einsum(
        "ysavuk,ytl->savuktl", columns, merid_tab, preferred_element_type=jnp.float32
    )
    real_part = products[:, :, :, 0, :, 0, :] + products[:, :, :, 1, :, 1, :]
    imag_part = products[:, :, :, 1, :, 0, :] - products[:, :, :, 0, :, 1, :]
    spectra = jnp.stack([real_part, imag_part]).astype(jnp.bfloat16)
    level_size = lax.axis_size("level")
    half_loop = level_size // 2
    own_index = lax.axis_index("level")
    blocks = [None] * level_size
    blocks[0] = cross_pair(spectra, spectra)
    partner = spectra
    for offset in range(1, half_loop + 1):
        partner = from_behind(partner, "level", 1)
        lower_pair = cross_pair(spectra, partner)
        blocks[level_size - offset] = lower_pair
        if offset < level_size - offset:
            blocks[offset] = from_behind(mirror(lower_pair), "level", -offset)
    assembled = jnp.stack(blocks, axis=3)
    assembled = jnp.roll(assembled, own_index * 1, axis=3)
    return assembled.reshape(2, var_count, lev_local, level_size * lev_local, wave_local, NL)


def solution(mesh):
    placed = (P("space", "level", None, None, None), P("space", "level", None, None, None))
    return jax.shard_map(
        on_device,
        mesh=mesh,
        in_specs=placed,
        out_specs=P(None, None, "level", None, "space", None),
        check_vma=False,
    )
```

profile of v0, /device:TPU:13, one launch (start us, length us, event | category | flops | bytes accessed | tf_op | source)
XLA Modules:
  0.0 237.3 jit_solution(5829251422824161080)
XLA Ops:
  0.0 0.1 iota_add_fusion
  0.1 12.9 %fusion.18 = (f32[1440,8,1,56]{0,3,2,1:T(8,128)S(1)}, f32[1440,8,1,56]{0,3,2,1:T(8,128)}) fusion(s32[8,56]{1,0:T(8,128)S(1)} %iota_add_fusion), kind=kLoop, calls=%fused_computation.30 | loop fusion | flops 6451200 | bytes 5162752 | tf_op jit(solution)/shard_map/cos | solution.py:28
  13.0 9.2 %fusion = bf16[88,8,3,1440,1,1]{3,1,2,0,5,4:T(8,128)(2,1)} fusion(bf16[88,1,8,3,1440]{4,2,3,1,0:T(8,128)(2,1)} %param.3, bf16[88,1,8,3,1440]{4,2,3,1,0:T(8,128)(2,1)} %param.2), kind=kLoop, calls=%fused_computation.1 | loop fusion | flops 12165120 | bytes 18247680 | tf_op jit(solution)/shard_map/reshape
  22.2 12.7 %convert_bitcast_fusion = bf16[88,8,8,1,3,2,56]{0,6,4,2,5,1,3:T(8,128)(2,1)S(1)} fusion(bf16[88,8,3,1440,1,1]{3,1,2,0,5,4:T(8,128)(2,1)} %fusion, f32[1440,8,1,56]{0,3,2,1:T(8,128)} %get-tuple-element.32, f32[1440,8,1,56]{0,3,2,1:T(8,128)S(1)} %get-tuple-element.31), kind=kOutput, calls=%fused_computation.6 | convolution fusion | flops 5455736832 | bytes 15028224 | tf_op jit(solution)/shard_map/yasvx,xpuk->ypsavuk/dot_general | solution.py:66
  34.9 3.4 %copy.18 = bf16[88,8,8,1,3,2,56]{0,6,5,4,2,1,3:T(8,128)(2,1)} copy(bf16[88,8,8,1,3,2,56]{0,6,4,2,5,1,3:T(8,128)(2,1)S(1)} %convert_bitcast_fusion) | data formatting | bytes 7569408 | tf_op jit(solution)/shard_map/convert_element_type | solution.py:68
  38.4 8.0 %copy.19 = bf16[88,8,8,336]{3,2,0,1:T(8,128)(2,1)} copy(bf16[88,8,8,336]{0,3,2,1:T(8,128)(2,1)} %bitcast.167) | data formatting | bytes 7569408 | tf_op jit(solution)/shard_map/reshape | solution.py:69
  46.4 5.7 %all-to-all-start = ((bf16[88,8,8,336]{3,2,0,1:T(8,128)(2,1)}), bf16[88,8,8,336]{3,2,0,1:T(8,128)(2,1)}, u32[]{:S(2)}, u32[]{:S(2)}) async-start(bf16[88,8,8,336]{3,2,0,1:T(8,128)(2,1)} %copy.19), calls=%async_computation | async-start | bytes 8650752 | tf_op jit(solution)/shard_map/all_to_all | solution.py:72
  52.1 4.4 %fusion.43 = (f32[704,1,384]{2,0,1:T(8,128)S(1)}, f32[704,1,384]{2,0,1:T(8,128)S(1)}) fusion(s32[384]{0:T(512)S(1)} %iota_add_fusion.1), kind=kLoop, calls=%fused_computation.62 | loop fusion | flops 2433024 | bytes 2164224 | tf_op jit(solution)/shard_map/cos | solution.py:37
  56.4 89.1 %all-to-all-done = bf16[88,8,8,336]{3,2,0,1:T(8,128)(2,1)} async-done(((bf16[88,8,8,336]{3,2,0,1:T(8,128)(2,1)}), bf16[88,8,8,336]{3,2,0,1:T(8,128)(2,1)}, u32[]{:S(2)}, u32[]{:S(2)}) %all-to-all-start) | async-done | bytes 3784736 | tf_op jit(solution)/shard_map/all_to_all | solution.py:72
  145.5 7.4 %copy.20 = bf16[8,88,1,8,336]{1,0,4,3,2:T(8,128)(2,1)} copy(bf16[8,88,1,8,336]{4,3,1,0,2:T(8,128)(2,1)} %bitcast.32) | data formatting | bytes 7569408 | tf_op jit(solution)/shard_map/all_to_all | solution.py:72
  152.9 9.5 %reshape.522 = bf16[704,8,3,2,56,1]{0,4,3,2,1,5:T(8,128)(2,1)} reshape(bf16[8,88,1,8,336]{1,0,4,3,2:T(8,128)(2,1)} %copy.20) | data formatting | bytes 7569408 | tf_op jit(solution)/shard_map/reshape.6
  162.4 5.3 %fusion.6 = f32[8,1,3,2,56,2,384]{6,4,5,3,2,0,1:T(8,128)S(1)} fusion(bf16[704,8,3,2,56,1]{0,4,3,2,1,5:T(8,128)(2,1)} %reshape.522, f32[704,1,384]{2,0,1:T(8,128)S(1)} %get-tuple-element.34, f32[704,1,384]{2,0,1:T(8,128)S(1)} %get-tuple-element.33), kind=kOutput, calls=%fused_computation.21 | convolution fusion | flops 2908274688 | bytes 14204928 | tf_op jit(solution)/shard_map/ysavuk,ytl->savuktl/dot_general | solution.py:75
  167.7 0.0 copy-start
  167.7 0.2 fusion.56
  167.9 0.3 fusion.57
  168.2 2.7 %copy-done = f32[8,1,3,2,56,2,384]{6,4,5,3,2,0,1:T(8,128)} copy-done((f32[8,1,3,2,56,2,384]{6,4,5,3,2,0,1:T(8,128)}, f32[8,1,3,2,56,2,384]{6,4,5,3,2,0,1:T(8,128)S(1)}, u32[]{:S(2)}) %copy-start) | copy-done | bytes 8257560
  170.9 0.2 pad_maximum_fusion
  171.1 1.6 collective-permute-start
  172.7 22.6 %collective-permute-done = bf16[2,8,1,3,56,384]{5,4,3,1,2,0:T(8,128)(2,1)S(1)} collective-permute-done((bf16[2,8,1,3,56,384]{5,4,3,1,2,0:T(8,128)(2,1)S(1)}, bf16[2,8,1,3,56,384]{5,4,3,1,2,0:T(8,128)(2,1)S(1)}, u32[]{:S(2)}, u32[]{:S(2)}) %collective-permute-start) | collective-permute-done | bytes 2064416 | tf_op jit(solution)/shard_map/ppermute | solution.py:16
  195.4 2.5 %collective-permute-start.2 = (bf16[2,8,1,3,56,384]{5,4,3,1,2,0:T(8,128)(2,1)S(1)}, bf16[2,8,1,3,56,384]{5,4,3,1,2,0:T(8,128)(2,1)}, u32[]{:S(2)}, u32[]{:S(2)}) collective-permute-start(bf16[2,8,1,3,56,384]{5,4,3,1,2,0:T(8,128)(2,1)S(1)} %collective-permute-done), channel_id=1, source_target_pairs={{24,0},{0,8},{8,16},{16,24},{25,1},{1,9},{9,17},{17,25},{26,2},{2,... | collective-permute-start | bytes 6193160 | tf_op jit(solution)/shard_map/ppermute | solution.py:16
  197.9 22.6 %collective-permute-done.2 = bf16[2,8,1,3,56,384]{5,4,3,1,2,0:T(8,128)(2,1)} collective-permute-done((bf16[2,8,1,3,56,384]{5,4,3,1,2,0:T(8,128)(2,1)S(1)}, bf16[2,8,1,3,56,384]{5,4,3,1,2,0:T(8,128)(2,1)}, u32[]{:S(2)}, u32[]{:S(2)}) %collective-permute-start.2) | collective-permute-done | bytes 2064416 | tf_op jit(solution)/shard_map/ppermute | solution.py:16
  220.5 5.4 %fusion.29 = (f32[3,56,384]{2,1,0:T(8,128)S(1)}, f32[3,56,384]{2,1,0:T(8,128)S(1)}, f32[3,56,384]{2,1,0:T(8,128)S(1)}, f32[3,56,384]{2,1,0:T(8,128)S(1)}, f32[3,...) fusion(bf16[2,8,1,3,56,384]{5,4,3,1,2,0:T(8,128)(2,1)S(1)} %col, ...), kind=kLoop, calls=%fused_computation.42 | loop fusion | flops 15805440 | bytes 15224832 | tf_op jit(solution)/shard_map/savkl,sbvkl->vabkl/dot_general | solution.py:46
  225.9 0.1 subtract_bitcast_fusion.2
  226.0 0.1 maximum_multiply_fusion.3
  226.1 1.5 collective-permute-start.1
  227.7 0.1 subtract_bitcast_fusion.1
  227.7 0.1 fusion.49
  227.8 0.1 subtract_bitcast_fusion
  227.9 7.7 %collective-permute-done.1 = f32[2,3,1,1,56,384]{5,4,1,3,2,0:T(8,128)S(1)} collective-permute-done((f32[2,3,1,1,56,384]{5,4,1,3,2,0:T(8,128)S(1)}, f32[2,3,1,1,56,384]{5,4,1,3,2,0:T(8,128)S(1)}, u32[]{:S(2)}, u32[]{:S(2)}) %collective-permute-start.1) | collective-permute-done | bytes 516128 | tf_op jit(solution)/shard_map/ppermute | solution.py:16
  235.8 1.4 dynamic-slice_bitcast_fusion
  (11 shorter events, 0.3 us)
Async XLA Ops:
  46.4 99.1 %all-to-all-start = ((bf16[88,8,8,336]{3,2,0,1:T(8,128)(2,1)}), bf16[88,8,8,336]{3,2,0,1:T(8,128)(2,1)}, u32[]{:S(2)}, u32[]{:S(2)}) async-start(bf16[88,8,8,336]{3,2,0,1:T(8,128)(2,1)} %copy.19), calls=%async_computation | async-start | bytes 8650752 | tf_op jit(solution)/shard_map/all_to_all | solution.py:72
  167.7 3.2 %copy-start = (f32[8,1,3,2,56,2,384]{6,4,5,3,2,0,1:T(8,128)}, f32[8,1,3,2,56,2,384]{6,4,5,3,2,0,1:T(8,128)S(1)}, u32[]{:S(2)}) copy-start(f32[8,1,3,2,56,2,384]{6,4,5,3,2,0,1:T(8,128)S(1)} %fusion.6) | copy-start | bytes 24772612
  171.1 24.3 %collective-permute-start = (bf16[2,8,1,3,56,384]{5,4,3,1,2,0:T(8,128)(2,1)S(1)}, bf16[2,8,1,3,56,384]{5,4,3,1,2,0:T(8,128)(2,1)S(1)}, u32[]{:S(2)}, u32[]{:S(2)}) collective-permute-start(bf16[2,8,1,3,56,384]{5,4,3,1,2,0:T(8,128)(2,1)S(1)} %pad_maximum_fusion), channel_id=1, source_target_pairs={{24,0},{0,8},{8,16},{16,24},{25,1},{1,9},{9,17},{17,25},{26,2},{2,... | collective-permute-start | bytes 6193160 | tf_op jit(solution)/shard_map/ppermute | solution.py:16
  195.4 25.1 %collective-permute-start.2 = (bf16[2,8,1,3,56,384]{5,4,3,1,2,0:T(8,128)(2,1)S(1)}, bf16[2,8,1,3,56,384]{5,4,3,1,2,0:T(8,128)(2,1)}, u32[]{:S(2)}, u32[]{:S(2)}) collective-permute-start(bf16[2,8,1,3,56,384]{5,4,3,1,2,0:T(8,128)(2,1)S(1)} %collective-permute-done), channel_id=1, source_target_pairs={{24,0},{0,8},{8,16},{16,24},{25,1},{1,9},{9,17},{17,25},{26,2},{2,... | collective-permute-start | bytes 6193160 | tf_op jit(solution)/shard_map/ppermute | solution.py:16
  226.1 9.4 %collective-permute-start.1 = (f32[2,3,1,1,56,384]{5,4,1,3,2,0:T(8,128)S(1)}, f32[2,3,1,1,56,384]{5,4,1,3,2,0:T(8,128)S(1)}, u32[]{:S(2)}, u32[]{:S(2)}) collective-permute-start(f32[2,3,1,1,56,384]{5,4,1,3,2,0:T(8,128)S(1)} %pad_maximum_fusion.1), channel_id=1, source_target_pairs={{8,0},{16,8},{24,16},{0,24},{9,1},{17,9},{25,17},{1,25},{10,2},{18... | collective-permute-start | bytes 1548296 | tf_op jit(solution)/shard_map/ppermute | solution.py:16
where the time goes:
time: 242 us; the launch traced here: 237 us
  waiting for transfers between devices  142 us (59%)
  other arithmetic  33.3 us (14%)
  local copies, waits for them, and re-layouts  32.5 us (13%)
  matrix products  18.1 us (7%)
  starting transfers between devices  11.3 us (5%)
    all_to_all x1, waiting for transfers between devices, on_device(): lax.all_to_all(zonal_coeff, 'space', split_axis=1, concat_axis=0, tiled=T...  89.1 us
    ppermute x3, waiting for transfers between devices, from_behind(): return lax.ppermute(block, axis, route)  52.9 us
    cos x1, other arithmetic, zonal_table(): jnp.cos(angle_rad)  12.9 us
    dot_general x1, matrix products, on_device(): jnp.einsum('yasvx,xpuk->ypsavuk', diff_field, zonal_tab, preferred_elemen...  12.7 us
    another operation x1, local copies, waits for them, and re-layouts  9.47 us
    reshape x1, other arithmetic  9.22 us
    reshape x1, local copies, waits for them, and re-layouts, on_device(): zonal_coeff.reshape(lat_local, space_size, sample_count, lev_local * var_...  8.04 us
    all_to_all x1, local copies, waits for them, and re-layouts, on_device(): lax.all_to_all(zonal_coeff, 'space', split_axis=1, concat_axis=0, tiled=T...  7.37 us
  transfers between devices with their start and end apart: 4, of which 4 were waited for; matrix products, arithmetic and copies ran while one was open for 2% of the time, Pallas kernels for 0%

commit v1 on v0

v1 whole, which is shorter than its diff:
```python
import math

import jax
import jax.numpy as jnp
import numpy as np
from jax import lax
from jax.sharding import PartitionSpec as P

MK = 448
NL = 384


def zonal_table(lon_size, wave_total):
    phase = np.arange(lon_size)[:, None] * np.arange(wave_total)[None, :] % lon_size
    angle = np.float32(2.0 * math.pi / lon_size) * phase.astype(np.float32)
    table = np.stack([np.cos(angle), -np.sin(angle)], axis=1) / np.float32(math.sqrt(lon_size))
    return table.astype(jnp.bfloat16)


def merid_table(lat_size, wave_total):
    wave_index = np.arange(wave_total) - wave_total // 2
    phase = np.arange(lat_size)[:, None] * wave_index[None, :] % lat_size
    angle = np.float32(2.0 * math.pi / lat_size) * phase.astype(np.float32)
    table = np.stack([np.cos(angle), np.sin(angle)], axis=1) / np.float32(math.sqrt(lat_size))
    return table.astype(jnp.bfloat16)


def swap_core(block, level_size):
    return lax.ppermute(block, "level", [(i, i ^ 1) for i in range(level_size)])


def from_chip(block, level_size, distance):
    return lax.ppermute(
        block, "level", [((i + 2 * distance) % level_size, i) for i in range(level_size)]
    )


def cross_pair(own_spec, other_spec):
    own = own_spec.astype(jnp.float32)
    other = other_spec.astype(jnp.float32)
    scale = 1.0 / own.shape[1]
    co_spec = (own[0] * other[0] + own[1] * other[1]).sum(axis=0) * scale
    quad_spec = (own[1] * other[0] - own[0] * other[1]).sum(axis=0) * scale
    return jnp.stack([co_spec, quad_spec])


def on_device(fc_long, fc_short):
    lat_local, lev_local, sample_count, var_count, lon_size = fc_long.shape
    space_size = lax.axis_size("space")
    level_size = lax.axis_size("level")
    wave_local = MK // space_size
    lat_total = lat_local * space_size
    zonal_tab = zonal_table(lon_size, MK).reshape(lon_size, 2, space_size, wave_local)
    zonal_tab = zonal_tab.transpose(0, 2, 1, 3)
    merid_tab = merid_table(lat_total, NL)
    core = lax.axis_index("level") % 2
    chip = lax.axis_index("level") // 2

    per_var = []
    for var in range(var_count):
        diff = (
            fc_long[:, 0, :, var].astype(jnp.float32) - fc_short[:, 0, :, var].astype(jnp.float32)
        ).astype(jnp.bfloat16)
        coeff = jnp.einsum(
            "ysx,xpuk->pysuk", diff, zonal_tab, preferred_element_type=jnp.float32
        ).astype(jnp.bfloat16)
        coeff = coeff.reshape(space_size * lat_local, sample_count * 2 * wave_local)
        columns = lax.all_to_all(coeff, "space", split_axis=0, concat_axis=0, tiled=True)
        products = jnp.einsum(
            "yn,ytl->ntl", columns, merid_tab, preferred_element_type=jnp.float32
        ).reshape(sample_count, 2, wave_local, 2, NL)
        real_part = products[:, 0, :, 0] + products[:, 1, :, 1]
        imag_part = products[:, 1, :, 0] - products[:, 0, :, 1]
        spectra = jnp.stack([real_part, imag_part]).astype(jnp.bfloat16)
        pairs = []
        for distance in range(level_size // 2):
            mine = spectra if distance == 0 else from_chip(spectra, level_size, distance)
            pairs.append((mine, swap_core(mine, level_size)))
        blocks = []
        for mine, mate in pairs:
            one = cross_pair(spectra, mine)
            two = cross_pair(spectra, mate)
            blocks.append(jnp.where(core == 0, one, two))
            blocks.append(jnp.where(core == 0, two, one))
        per_var.append(jnp.stack(blocks, axis=1))
    assembled = jnp.stack(per_var, axis=1)
    assembled = jnp.roll(assembled, 2 * chip, axis=2)
    return assembled[:, :, None]


def solution(mesh):
    placed = (P("space", "level", None, None, None), P("space", "level", None, None, None))
    return jax.shard_map(
        on_device,
        mesh=mesh,
        in_specs=placed,
        out_specs=P(None, None, "level", None, "space", None),
        check_vma=False,
    )
```

time: 242 us -> 157 us (0.65)
  waiting for transfers between devices: 142 us -> 50.7 us
  other arithmetic: 33.3 us -> 15.8 us
  starting transfers between devices: 11.3 us -> 27.9 us
  matrix products: 18.1 us -> 33.9 us
  local copies, waits for them, and re-layouts: 32.5 us -> 25.9 us
    all_to_all x1 -> x3, waiting for transfers between devices: 89.1 us -> 39.5 us  [on_device(): lax.all_to_all(coeff, 'space', split_axis=0, concat_axis=0, tiled=True)]
    ppermute x3 -> x9, waiting for transfers between devices: 52.9 us -> 11.2 us  [the longest x3 11.2 us: from_chip(): lax.ppermute(block, 'level', [((i + 2 * distance) % level_size, i) for i...]
    cos x2 -> x0, other arithmetic: 17.3 us -> none  [the longest x1 12.9 us: zonal_table(): jnp.cos(angle_rad)]
    dot_general x2 -> x6, matrix products: 18.1 us -> 33.9 us  [the longest x3 25.2 us: on_device(): jnp.einsum('ysx,xpuk->pysuk', diff, zonal_tab, preferred_element_type=jnp...]
    all_to_all x1 -> x3, starting transfers between devices: 5.66 us -> 18.4 us  [on_device(): lax.all_to_all(coeff, 'space', split_axis=0, concat_axis=0, tiled=True)]
    convert_element_type x0 -> x12, other arithmetic: none -> 11 us  [the longest x9 7.52 us: cross_pair(): other = other_spec.astype(jnp.float32)]
    convert_element_type x1 -> x3, local copies, waits for them, and re-layouts: 3.41 us -> 13.3 us  [on_device(): coeff = jnp.einsum('ysx,xpuk->pysuk', diff, zonal_tab, preferred_element_...]
    reshape x2 -> x0, local copies, waits for them, and re-layouts: 9.49 us -> none  [the longest x1 8.04 us: on_device(): zonal_coeff.reshape(lat_local, space_size, sample_count, lev_local * var_...]
  transfers between devices with their start and end apart: 4 -> 12, of which waited for: 4 -> 5; matrix products, arithmetic and copies ran while one was open for 2% -> 37% of each run, Pallas kernels for 0% -> 0%
where the time goes in v1:
time: 157 us; the launch traced here: 155 us
  waiting for transfers between devices  50.7 us (32%)
  matrix products  33.9 us (22%)
  starting transfers between devices  27.9 us (18%)
  local copies, waits for them, and re-layouts  25.9 us (16%)
  other arithmetic  15.8 us (10%)
    all_to_all x3, waiting for transfers between devices, on_device(): lax.all_to_all(coeff, 'space', split_axis=0, concat_axis=0, tiled=True)  39.5 us
    dot_general x3, matrix products, on_device(): jnp.einsum('ysx,xpuk->pysuk', diff, zonal_tab, preferred_element_type=jnp...  25.2 us
    all_to_all x3, starting transfers between devices, on_device(): lax.all_to_all(coeff, 'space', split_axis=0, concat_axis=0, tiled=True)  18.4 us
    convert_element_type x3, local copies, waits for them, and re-layouts, on_device(): coeff = jnp.einsum('ysx,xpuk->pysuk', diff, zonal_tab, preferred_element_...  13.3 us
    ppermute x3, waiting for transfers between devices, from_chip(): lax.ppermute(block, 'level', [((i + 2 * distance) % level_size, i) for i...  11.2 us
    dot_general x3, matrix products, on_device(): jnp.einsum('yn,ytl->ntl', columns, merid_tab, preferred_element_type=jnp....  8.68 us
    convert_element_type x9, other arithmetic, cross_pair(): other = other_spec.astype(jnp.float32)  7.52 us
    ppermute x6, starting transfers between devices, swap_core(): return lax.ppermute(block, 'level', [(i, i ^ 1) for i in range(level_size)])  6.89 us
  transfers between devices with their start and end apart: 12, of which 5 were waited for; matrix products, arithmetic and copies ran while one was open for 37% of the time, Pallas kernels for 0%

profile of v1, /device:TPU:13, one launch (start us, length us, event | category | flops | bytes accessed | tf_op | source)
XLA Modules:
  0.0 154.7 jit_solution(743119629438248830)
XLA Ops:
  0.0 8.4 %convert_bitcast_fusion.2 = bf16[8,88,8,2,56]{4,2,3,0,1:T(8,128)(2,1)} fusion(bf16[1440,8,2,56,1]{0,3,2,1,4:T(8,128)(2,1)} %constant.63, bf16[88,1,8,3,1440]{4,2,3,1,0:T(8,128)(2,1)} %param.9, bf16[88,1,8,3,1440]{4,2,3,1,0:T(8,128)(2,1)} %param.8), kind=kOutput, calls=%fused_computation.11 | convolution fusion | flops 1821343744 | bytes 8339456 | tf_op jit(solution)/shard_map/ysx,xpuk->pysuk/dot_general | solution.py:64
  8.4 4.4 %copy.34 = bf16[8,88,8,2,56]{1,4,3,2,0:T(8,128)(2,1)S(1)} copy(bf16[8,88,8,2,56]{4,2,3,0,1:T(8,128)(2,1)} %convert_bitcast_fusion.2) | data formatting | bytes 2523136 | tf_op jit(solution)/shard_map/convert_element_type | solution.py:66
  12.8 1.6 %copy.35 = bf16[8,88,896]{2,1,0:T(8,128)(2,1)} copy(bf16[8,88,896]{1,2,0:T(8,128)(2,1)S(1)} %bitcast.181) | data formatting | bytes 2523136 | tf_op jit(solution)/shard_map/all_to_all | solution.py:68
  14.4 5.7 %all-to-all-start = ((bf16[8,88,896]{2,1,0:T(8,128)(2,1)}), bf16[8,88,896]{2,1,0:T(8,128)(2,1)S(1)}, u32[]{:S(2)}, u32[]{:S(2)}) async-start(bf16[8,88,896]{2,1,0:T(8,128)(2,1)} %copy.35), calls=%async_computation | async-start | bytes 2523136 | tf_op jit(solution)/shard_map/all_to_all | solution.py:68
  20.1 8.4 %convert_bitcast_fusion = bf16[8,88,8,2,56]{4,2,3,0,1:T(8,128)(2,1)} fusion(bf16[1440,8,2,56,1]{0,3,2,1,4:T(8,128)(2,1)} %constant.63, bf16[88,1,8,3,1440]{4,2,3,1,0:T(8,128)(2,1)} %param.9, bf16[88,1,8,3,1440]{4,2,3,1,0:T(8,128)(2,1)} %param.8), kind=kOutput, calls=%fused_computation.9 | convolution fusion | flops 1821343744 | bytes 8339456 | tf_op jit(solution)/shard_map/ysx,xpuk->pysuk/dot_general | solution.py:64
  28.5 4.4 %copy.44 = bf16[8,88,8,2,56]{1,4,3,2,0:T(8,128)(2,1)S(1)} copy(bf16[8,88,8,2,56]{4,2,3,0,1:T(8,128)(2,1)} %convert_bitcast_fusion) | data formatting | bytes 2523136 | tf_op jit(solution)/shard_map/convert_element_type | solution.py:66
  32.9 1.6 %copy.45 = bf16[8,88,896]{2,1,0:T(8,128)(2,1)} copy(bf16[8,88,896]{1,2,0:T(8,128)(2,1)S(1)} %bitcast.182) | data formatting | bytes 2523136 | tf_op jit(solution)/shard_map/all_to_all | solution.py:68
  34.5 13.4 %all-to-all-done = bf16[8,88,896]{2,1,0:T(8,128)(2,1)S(1)} async-done(((bf16[8,88,896]{2,1,0:T(8,128)(2,1)}), bf16[8,88,896]{2,1,0:T(8,128)(2,1)S(1)}, u32[]{:S(2)}, u32[]{:S(2)}) %all-to-all-start) | async-done | bytes 1261600 | tf_op jit(solution)/shard_map/all_to_all | solution.py:68
  47.9 1.0 copy-done.2
  48.9 6.3 %all-to-all-start.2 = ((bf16[8,88,896]{2,1,0:T(8,128)(2,1)}), bf16[8,88,896]{2,1,0:T(8,128)(2,1)S(1)}, u32[]{:S(2)}, u32[]{:S(2)}) async-start(bf16[8,88,896]{2,1,0:T(8,128)(2,1)} %copy.45), calls=%async_computation.2 | async-start | bytes 2523136 | tf_op jit(solution)/shard_map/all_to_all | solution.py:68
  55.3 8.4 %convert_bitcast_fusion.1 = bf16[8,88,8,2,56]{4,2,3,0,1:T(8,128)(2,1)} fusion(bf16[1440,8,2,56,1]{0,3,2,1,4:T(8,128)(2,1)} %constant.63, bf16[88,1,8,3,1440]{4,2,3,1,0:T(8,128)(2,1)} %param.9, bf16[88,1,8,3,1440]{4,2,3,1,0:T(8,128)(2,1)} %param.8), kind=kOutput, calls=%fused_computation.10 | convolution fusion | flops 1821343744 | bytes 8339456 | tf_op jit(solution)/shard_map/ysx,xpuk->pysuk/dot_general | solution.py:64
  63.7 4.4 %copy.39 = bf16[8,88,8,2,56]{1,4,3,2,0:T(8,128)(2,1)S(1)} copy(bf16[8,88,8,2,56]{4,2,3,0,1:T(8,128)(2,1)} %convert_bitcast_fusion.1) | data formatting | bytes 2523136 | tf_op jit(solution)/shard_map/convert_element_type | solution.py:66
  68.1 1.6 %copy.40 = bf16[8,88,896]{2,1,0:T(8,128)(2,1)} copy(bf16[8,88,896]{1,2,0:T(8,128)(2,1)S(1)} %bitcast.183) | data formatting | bytes 2523136 | tf_op jit(solution)/shard_map/all_to_all | solution.py:68
  69.7 13.4 %all-to-all-done.2 = bf16[8,88,896]{2,1,0:T(8,128)(2,1)S(1)} async-done(((bf16[8,88,896]{2,1,0:T(8,128)(2,1)}), bf16[8,88,896]{2,1,0:T(8,128)(2,1)S(1)}, u32[]{:S(2)}, u32[]{:S(2)}) %all-to-all-start.2) | async-done | bytes 1261600 | tf_op jit(solution)/shard_map/all_to_all | solution.py:68
  83.1 6.3 %all-to-all-start.1 = ((bf16[8,88,896]{2,1,0:T(8,128)(2,1)}), bf16[8,88,896]{2,1,0:T(8,128)(2,1)S(1)}, u32[]{:S(2)}, u32[]{:S(2)}) async-start(bf16[8,88,896]{2,1,0:T(8,128)(2,1)} %copy.40), calls=%async_computation.1 | async-start | bytes 2523136 | tf_op jit(solution)/shard_map/all_to_all | solution.py:68
  89.4 2.5 %copy.36 = bf16[896,704]{1,0:T(8,128)(2,1)} copy(bf16[896,704]{0,1:T(8,128)(2,1)} %bitcast.186) | data formatting | bytes 2523136 | tf_op jit(solution)/shard_map/yn,ytl->ntl/dot_general | solution.py:69
  91.9 2.9 %fusion.48 = f32[8,2,56,2,384]{4,2,3,1,0:T(8,128)S(1)} fusion(bf16[8,2,56,704,1]{3,2,4,1,0:T(8,128)(2,1)} %bitcast.188, bf16[704,2,384,1,1]{2,0,1,4,3:T(8,128)(2,1)} %constant.64), kind=kOutput, calls=%fused_computation.132 | convolution fusion | flops 968884224 | bytes 5095424 | tf_op jit(solution)/shard_map/yn,ytl->ntl/dot_general | solution.py:69
  94.8 0.1 fusion.28
  94.9 0.1 fusion.27
  95.0 1.0 fusion.47
  96.0 1.2 collective-permute-start.1
  97.2 2.5 %copy.46 = bf16[896,704]{1,0:T(8,128)(2,1)} copy(bf16[896,704]{0,1:T(8,128)(2,1)} %bitcast.185) | data formatting | bytes 2523136 | tf_op jit(solution)/shard_map/yn,ytl->ntl/dot_general | solution.py:69
  99.7 2.9 %fusion.50 = f32[8,2,56,2,384]{4,2,3,1,0:T(8,128)S(1)} fusion(bf16[8,2,56,704,1]{3,2,4,1,0:T(8,128)(2,1)} %bitcast.189, bf16[704,2,384,1,1]{2,0,1,4,3:T(8,128)(2,1)} %constant.64), kind=kOutput, calls=%fused_computation.134 | convolution fusion | flops 968884224 | bytes 5095424 | tf_op jit(solution)/shard_map/yn,ytl->ntl/dot_general | solution.py:69
  102.6 0.1 fusion.32
  102.7 0.1 fusion.31
  102.8 1.5 fusion.45
  104.2 0.3 collective-permute-start.7
  104.5 12.7 %all-to-all-done.1 = bf16[8,88,896]{2,1,0:T(8,128)(2,1)S(1)} async-done(((bf16[8,88,896]{2,1,0:T(8,128)(2,1)}), bf16[8,88,896]{2,1,0:T(8,128)(2,1)S(1)}, u32[]{:S(2)}, u32[]{:S(2)}) %all-to-all-start.1) | async-done | bytes 1261600 | tf_op jit(solution)/shard_map/all_to_all | solution.py:68
  117.2 1.9 %copy.41 = bf16[896,704]{1,0:T(8,128)(2,1)} copy(bf16[896,704]{0,1:T(8,128)(2,1)S(1)} %bitcast.184) | data formatting | bytes 2523136 | tf_op jit(solution)/shard_map/yn,ytl->ntl/dot_general | solution.py:69
  119.1 2.9 %fusion.49 = f32[8,2,56,2,384]{4,2,3,1,0:T(8,128)S(1)} fusion(bf16[8,2,56,704,1]{3,2,4,1,0:T(8,128)(2,1)} %bitcast.187, bf16[704,2,384,1,1]{2,0,1,4,3:T(8,128)(2,1)} %constant.64), kind=kOutput, calls=%fused_computation.133 | convolution fusion | flops 968884224 | bytes 5095424 | tf_op jit(solution)/shard_map/yn,ytl->ntl/dot_general | solution.py:69
  122.0 0.1 fusion.30
  122.1 0.1 fusion.29
  122.2 1.0 fusion.46
  123.2 1.2 collective-permute-start.4
  124.4 0.8 collective-permute-start
  125.1 0.0 collective-permute-start.6
  125.2 0.0 collective-permute-done.1
  125.2 0.5 collective-permute-start.3
  125.7 1.3 collective-permute-done.7
  126.9 3.6 %collective-permute-start.8 = (bf16[2,8,56,384]{3,2,1,0:T(8,128)(2,1)}, bf16[2,8,56,384]{3,2,1,0:T(8,128)(2,1)}, u32[]{:S(2)}, u32[]{:S(2)}) collective-permute-start(bf16[2,8,56,384]{3,2,1,0:T(8,128)(2,1)} %collective-permute-done.7), channel_id=1, source_target_pairs={{0,8},{8,0},{16,24},{24,16},{1,9},{9,1},{17,25},{25,17},{2,10},{10... | collective-permute-start | bytes 2064392 | tf_op jit(solution)/shard_map/ppermute | solution.py:29
  130.5 1.2 convert_element_type.139
  131.7 0.1 convert_element_type.119
  131.8 9.9 %collective-permute-done.4 = bf16[2,8,56,384]{3,2,1,0:T(8,128)(2,1)} collective-permute-done((bf16[2,8,56,384]{3,2,1,0:T(8,128)(2,1)}, bf16[2,8,56,384]{3,2,1,0:T(8,128)(2,1)}, u32[]{:S(2)}, u32[]{:S(2)}) %collective-permute-start.4) | collective-permute-done | bytes 688160 | tf_op jit(solution)/shard_map/ppermute | solution.py:33
  141.7 2.0 %collective-permute-start.2 = (bf16[2,8,56,384]{3,2,1,0:T(8,128)(2,1)S(1)}, bf16[2,8,56,384]{3,2,1,0:T(8,128)(2,1)S(1)}, u32[]{:S(2)}, u32[]{:S(2)}) collective-permute-start(bf16[2,8,56,384]{3,2,1,0:T(8,128)(2,1)S(1)} %collective-permute-done.1), channel_id=1, source_target_pairs={{0,8},{8,0},{16,24},{24,16},{1,9},{9,1},{17,25},{25,17},{2,10},{10... | collective-permute-start | bytes 2064392 | tf_op jit(solution)/shard_map/ppermute | solution.py:29
  143.7 1.2 convert_element_type.129
  144.9 0.0 collective-permute-done
  144.9 0.1 collective-permute-start.5
  144.9 1.2 convert_element_type.118
  146.1 0.0 collective-permute-done.6
  146.1 1.2 convert_element_type.138
  147.3 0.0 collective-permute-done.3
  147.4 1.3 convert_element_type.128
  148.7 0.0 collective-permute-done.8
  148.7 1.2 convert_element_type.140
  149.9 0.7 add_reduce_fusion.2
  150.7 0.0 collective-permute-done.5
  150.7 0.1 convert_element_type.130
  150.8 0.7 add_reduce_fusion.6
  151.7 0.1 convert_element_type.120
  151.8 0.7 add_reduce_fusion.10
  152.8 0.1 maximum_bitcast_fusion
  152.8 0.1 fusion.34
  152.9 0.1 fusion.38
  153.1 1.6 %fusion.15 = f32[2,3,1,4,56,384]{5,4,3,2,1,0:T(8,128)} fusion(s32[]{:T(128)S(6)} %select_n.175, f32[2,1,4,56,384]{4,3,2,1,0:T(8,128)S(1)} %maximum_bitcast_fusion, f32[2,1,4,56,384]{4,3,2,1,0:T(8,128)S(1)} %maximum_bitcast_fusion.1, f32[2,1,4,56,384]{4,3,2,1,0:T(8,128)S(1)} %maximum_bitcast_fusion.2), kind=kLoop, calls=%fused_computation.24 | loop fusion | flops 2580480 | bytes 4128772 | tf_op jit(solution)/shard_map/broadcast_in_dim | solution.py:88
  (30 shorter events, 0.4 us)
Async XLA Ops:
  14.4 33.5 %all-to-all-start = ((bf16[8,88,896]{2,1,0:T(8,128)(2,1)}), bf16[8,88,896]{2,1,0:T(8,128)(2,1)S(1)}, u32[]{:S(2)}, u32[]{:S(2)}) async-start(bf16[8,88,896]{2,1,0:T(8,128)(2,1)} %copy.35), calls=%async_computation | async-start | bytes 2523136 | tf_op jit(solution)/shard_map/all_to_all | solution.py:68
  47.9 1.0 copy-start.2
  48.9 34.2 %all-to-all-start.2 = ((bf16[8,88,896]{2,1,0:T(8,128)(2,1)}), bf16[8,88,896]{2,1,0:T(8,128)(2,1)S(1)}, u32[]{:S(2)}, u32[]{:S(2)}) async-start(bf16[8,88,896]{2,1,0:T(8,128)(2,1)} %copy.45), calls=%async_computation.2 | async-start | bytes 2523136 | tf_op jit(solution)/shard_map/all_to_all | solution.py:68
  83.1 11.8 %copy-start.1 = (bf16[8,88,896]{2,1,0:T(8,128)(2,1)}, bf16[8,88,896]{2,1,0:T(8,128)(2,1)S(1)}, u32[]{:S(2)}) copy-start(bf16[8,88,896]{2,1,0:T(8,128)(2,1)S(1)} %all-to-all-done.2) | copy-start | bytes 3784708
  83.1 34.2 %all-to-all-start.1 = ((bf16[8,88,896]{2,1,0:T(8,128)(2,1)}), bf16[8,88,896]{2,1,0:T(8,128)(2,1)S(1)}, u32[]{:S(2)}, u32[]{:S(2)}) async-start(bf16[8,88,896]{2,1,0:T(8,128)(2,1)} %copy.40), calls=%async_computation.1 | async-start | bytes 2523136 | tf_op jit(solution)/shard_map/all_to_all | solution.py:68
  96.0 29.2 %collective-permute-start.1 = (bf16[2,8,56,384]{3,2,1,0:T(8,128)(2,1)}, bf16[2,8,56,384]{3,2,1,0:T(8,128)(2,1)S(1)}, u32[]{:S(2)}, u32[]{:S(2)}) collective-permute-start(bf16[2,8,56,384]{3,2,1,0:T(8,128)(2,1)} %get-tuple-element.52), channel_id=1, source_target_pairs={{16,0},{24,8},{0,16},{8,24},{17,1},{25,9},{1,17},{9,25},{18,2},{26... | collective-permute-start | bytes 2064392 | tf_op jit(solution)/shard_map/ppermute | solution.py:33
  104.2 22.7 %collective-permute-start.7 = (bf16[2,8,56,384]{3,2,1,0:T(8,128)(2,1)}, bf16[2,8,56,384]{3,2,1,0:T(8,128)(2,1)}, u32[]{:S(2)}, u32[]{:S(2)}) collective-permute-start(bf16[2,8,56,384]{3,2,1,0:T(8,128)(2,1)} %get-tuple-element.48), channel_id=1, source_target_pairs={{16,0},{24,8},{0,16},{8,24},{17,1},{25,9},{1,17},{9,25},{18,2},{26... | collective-permute-start | bytes 2064392 | tf_op jit(solution)/shard_map/ppermute | solution.py:33
  123.2 18.5 %collective-permute-start.4 = (bf16[2,8,56,384]{3,2,1,0:T(8,128)(2,1)}, bf16[2,8,56,384]{3,2,1,0:T(8,128)(2,1)}, u32[]{:S(2)}, u32[]{:S(2)}) collective-permute-start(bf16[2,8,56,384]{3,2,1,0:T(8,128)(2,1)} %get-tuple-element.50), channel_id=1, source_target_pairs={{16,0},{24,8},{0,16},{8,24},{17,1},{25,9},{1,17},{9,25},{18,2},{26... | collective-permute-start | bytes 2064392 | tf_op jit(solution)/shard_map/ppermute | solution.py:33
  124.4 20.5 %collective-permute-start = (bf16[2,8,56,384]{3,2,1,0:T(8,128)(2,1)}, bf16[2,8,56,384]{3,2,1,0:T(8,128)(2,1)}, u32[]{:S(2)}, u32[]{:S(2)}) collective-permute-start(bf16[2,8,56,384]{3,2,1,0:T(8,128)(2,1)} %get-tuple-element.52), channel_id=1, source_target_pairs={{0,8},{8,0},{16,24},{24,16},{1,9},{9,1},{17,25},{25,17},{2,10},{10... | collective-permute-start | bytes 2064392 | tf_op jit(solution)/shard_map/ppermute | solution.py:29
  125.1 21.0 %collective-permute-start.6 = (bf16[2,8,56,384]{3,2,1,0:T(8,128)(2,1)}, bf16[2,8,56,384]{3,2,1,0:T(8,128)(2,1)}, u32[]{:S(2)}, u32[]{:S(2)}) collective-permute-start(bf16[2,8,56,384]{3,2,1,0:T(8,128)(2,1)} %get-tuple-element.48), channel_id=1, source_target_pairs={{0,8},{8,0},{16,24},{24,16},{1,9},{9,1},{17,25},{25,17},{2,10},{10... | collective-permute-start | bytes 2064392 | tf_op jit(solution)/shard_map/ppermute | solution.py:29
  125.2 22.2 %collective-permute-start.3 = (bf16[2,8,56,384]{3,2,1,0:T(8,128)(2,1)}, bf16[2,8,56,384]{3,2,1,0:T(8,128)(2,1)}, u32[]{:S(2)}, u32[]{:S(2)}) collective-permute-start(bf16[2,8,56,384]{3,2,1,0:T(8,128)(2,1)} %get-tuple-element.50), channel_id=1, source_target_pairs={{0,8},{8,0},{16,24},{24,16},{1,9},{9,1},{17,25},{25,17},{2,10},{10... | collective-permute-start | bytes 2064392 | tf_op jit(solution)/shard_map/ppermute | solution.py:29
  126.9 21.7 %collective-permute-start.8 = (bf16[2,8,56,384]{3,2,1,0:T(8,128)(2,1)}, bf16[2,8,56,384]{3,2,1,0:T(8,128)(2,1)}, u32[]{:S(2)}, u32[]{:S(2)}) collective-permute-start(bf16[2,8,56,384]{3,2,1,0:T(8,128)(2,1)} %collective-permute-done.7), channel_id=1, source_target_pairs={{0,8},{8,0},{16,24},{24,16},{1,9},{9,1},{17,25},{25,17},{2,10},{10... | collective-permute-start | bytes 2064392 | tf_op jit(solution)/shard_map/ppermute | solution.py:29
  141.7 10.1 %collective-permute-start.2 = (bf16[2,8,56,384]{3,2,1,0:T(8,128)(2,1)S(1)}, bf16[2,8,56,384]{3,2,1,0:T(8,128)(2,1)S(1)}, u32[]{:S(2)}, u32[]{:S(2)}) collective-permute-start(bf16[2,8,56,384]{3,2,1,0:T(8,128)(2,1)S(1)} %collective-permute-done.1), channel_id=1, source_target_pairs={{0,8},{8,0},{16,24},{24,16},{1,9},{9,1},{17,25},{25,17},{2,10},{10... | collective-permute-start | bytes 2064392 | tf_op jit(solution)/shard_map/ppermute | solution.py:29
  144.9 5.9 %collective-permute-start.5 = (bf16[2,8,56,384]{3,2,1,0:T(8,128)(2,1)}, bf16[2,8,56,384]{3,2,1,0:T(8,128)(2,1)S(1)}, u32[]{:S(2)}, u32[]{:S(2)}) collective-permute-start(bf16[2,8,56,384]{3,2,1,0:T(8,128)(2,1)} %collective-permute-done.4), channel_id=1, source_target_pairs={{0,8},{8,0},{16,24},{24,16},{1,9},{9,1},{17,25},{25,17},{2,10},{10... | collective-permute-start | bytes 2064392 | tf_op jit(solution)/shard_map/ppermute | solution.py:29
  147.3 2.5 %copy-start = (f32[2,8,56,384]{3,2,1,0:T(8,128)S(1)}, f32[2,8,56,384]{3,2,1,0:T(8,128)}, u32[]{:S(2)}) copy-start(f32[2,8,56,384]{3,2,1,0:T(8,128)} %get-tuple-element.47) | copy-start | bytes 4128772

commit v2 on v1

--- a/solution.py
+++ b/solution.py
@@ -1,9 +1,12 @@
+import functools
 import math
 
 import jax
 import jax.numpy as jnp
 import numpy as np
 from jax import lax
+from jax.experimental import pallas as pl
+from jax.experimental.pallas import tpu as pltpu
 from jax.sharding import PartitionSpec as P
 
 MK = 448
@@ -44,7 +47,7 @@
     return jnp.stack([co_spec, quad_spec])
 
 
-def on_device(fc_long, fc_short):
+def by_collectives(fc_long, fc_short):
     lat_local, lev_local, sample_count, var_count, lon_size = fc_long.shape
     space_size = lax.axis_size("space")
     level_size = lax.axis_size("level")
@@ -88,6 +91,275 @@
     return assembled[:, :, None]
 
 
+LANES = 128
+MESH = pl.DeviceIdType.MESH
+BLOCKS = (
+    ((0, 6), (1, 6), 6, 1, 0),
+    ((0, 0), (1, 0), 0, 2, 0),
+    ((0, 2), (1, 2), 2, 2, 0),
+    ((0, 4), (1, 4), 4, 2, 0),
+    ((2, 0), (2, 4), 7, 2, 1),
+    ((2, 2), (2, 6), 9, 2, 1),
+)
+ORDER = (1, 2, 3, 4, 5, 0)
+TILES = 11
+
+
+def kernel(
+    space_size, lat, wave, diff_ref, tab_ref, merid_ref, out_ref,
+    send, recv, spec, last, acc,
+    a2a_send, a2a_recv, own_sem, mate_send, mate_recv, far_send, far_recv, fwd_send, fwd_recv,
+):
+    me = lax.axis_index("space")
+    level = lax.axis_index("level")
+    mate = level + 1 - 2 * lax.rem(level, 2)
+    far = lax.rem(level + 2, 4)
+    far_mate = lax.rem(mate + 2, 4)
+    rows = 2 * lat
+    half = NL
+    own_rows = pl.ds(pl.multiple_of(me * rows, 16), rows)
+
+    barrier = pltpu.get_barrier_semaphore()
+    for d in range(1, space_size):
+        peer = lax.rem(me + d, space_size)
+        pl.semaphore_signal(barrier, inc=1, device_id={"space": peer}, device_id_type=MESH)
+    for peer in (mate, far):
+        pl.semaphore_signal(barrier, inc=1, device_id={"level": peer}, device_id_type=MESH)
+
+    def columns(block):
+        first, count = BLOCKS[block][2:4]
+        return pl.ds(first * LANES, count * LANES)
+
+    def to_peer(block, d):
+        peer = lax.rem(me + d, space_size)
+        cols = columns(block)
+        return pltpu.make_async_remote_copy(
+            src_ref=send.at[peer, :, cols],
+            dst_ref=recv.at[own_rows, cols],
+            send_sem=a2a_send.at[block, d],
+            recv_sem=a2a_recv.at[block, d],
+            device_id={"space": peer},
+            device_id_type=MESH,
+        )
+
+    def to_self(block):
+        cols = columns(block)
+        return pltpu.make_async_copy(
+            send.at[me, :, cols], recv.at[own_rows, cols], own_sem.at[block]
+        )
+
+    def to_level(block, peer, source, slot, send_sem, recv_sem):
+        cols = columns(block)
+        return pltpu.make_async_remote_copy(
+            src_ref=spec.at[source, :, cols],
+            dst_ref=spec.at[slot, :, cols],
+            send_sem=send_sem.at[block],
+            recv_sem=recv_sem.at[block],
+            device_id={"level": peer},
+            device_id_type=MESH,
+        )
+
+    def to_mate(block):
+        return to_level(block, mate, 0, 1, mate_send, mate_recv)
+
+    def to_far(block):
+        return to_level(block, far, 0, 2, far_send, far_recv)
+
+    def forward(block):
+        return to_level(block, mate, 2, 3, fwd_send, fwd_recv)
+
+    def zonal(block, d):
+        (var0, s0), (var1, s1), first, count, group = BLOCKS[block]
+        peer = lax.rem(me + d, space_size)
+        samples = 8
+        start0 = (var0 * samples + s0) * lat
+        start1 = (var1 * samples + s1) * lat
+        z = jnp.dot(
+            diff_ref[start0 : start0 + rows, :], tab_ref[0, peer],
+            preferred_element_type=jnp.float32,
+        ) + jnp.dot(
+            diff_ref[start1 : start1 + rows, :], tab_ref[1, peer],
+            preferred_element_type=jnp.float32,
+        )
+        lane = lax.broadcasted_iota(jnp.int32, (rows, LANES), 1)
+        tiles = [
+            jnp.concatenate([z[i * lat : (i + 1) * lat, :LANES], z[i * lat : (i + 1) * lat, LANES:]], axis=0)
+            for i in range(2)
+        ]
+        if count == 1:
+            last[peer] = tiles[1]
+        for i in range(count):
+            tile = tiles[i]
+            if group == 0:
+                t = first + i
+                extra = pltpu.roll(last[peer], 2 * wave - 16 * t, 1)
+                tile = jnp.where(lane < 2 * wave, tile, extra)
+            send[peer, :, (first + i) * LANES : (first + i + 1) * LANES] = tile.astype(jnp.bfloat16)
+
+    for block in range(len(BLOCKS)):
+        def one_peer(step, carry, block=block):
+            d = step + 1
+
+            @pl.when(d < space_size)
+            def _():
+                zonal(block, d)
+                if block > 0:
+                    to_peer(block, d).start()
+
+            return carry
+
+        if block == 1:
+            pl.semaphore_wait(barrier, space_size + 1)
+        lax.fori_loop(0, space_size - 1, one_peer, 0)
+        zonal(block, 0)
+        to_self(block).start()
+    for d in range(1, space_size):
+        to_peer(0, d).start()
+
+    def meridional(block):
+        first, count = BLOCKS[block][2:4]
+        cols = slice(first * LANES, (first + count) * LANES)
+        for d in range(1, space_size):
+            to_peer(block, d).wait_recv()
+        to_self(block).wait()
+
+        def part(r, carry):
+            r_rows = pl.ds(pl.multiple_of(r * 256, 256), 256)
+            total = jnp.dot(merid_ref[r_rows, :], recv[:, cols], preferred_element_type=jnp.float32)
+            spec[0, r_rows, cols] = total.astype(jnp.bfloat16)
+            return carry
+
+        lax.fori_loop(0, 2 * half // 256, part, 0)
+
+    def cross(block):
+        first, count, group = BLOCKS[block][2:]
+        fresh = block in (1, 4)
+        step_rows = 32
+
+        def part(r, carry):
+            base = pl.multiple_of(r * step_rows, step_rows)
+            re_rows = pl.ds(base, step_rows)
+            im_rows = pl.ds(pl.multiple_of(half + r * step_rows, step_rows), step_rows)
+            lane = lax.broadcasted_iota(jnp.int32, (step_rows, LANES), 1)
+            for slot in range(4):
+                co_sum = None
+                for i in range(count):
+                    t = first + i
+                    cols = slice(t * LANES, (t + 1) * LANES)
+                    a_re = spec[0, re_rows, cols].astype(jnp.float32)
+                    a_im = spec[0, im_rows, cols].astype(jnp.float32)
+                    b_re = spec[slot, re_rows, cols].astype(jnp.float32)
+                    b_im = spec[slot, im_rows, cols].astype(jnp.float32)
+                    co = a_re * b_re + a_im * b_im
+                    quad = a_im * b_re - a_re * b_im
+                    if group == 0:
+                        here = (lane >= 16 * t) & (lane < 16 * t + 16)
+                        shift = (16 * t + 16) % LANES
+                        co = co + jnp.where(here, pltpu.roll(co, shift, 1), 0.0)
+                        quad = quad + jnp.where(here, pltpu.roll(quad, shift, 1), 0.0)
+                    co_sum = co if co_sum is None else co_sum + co
+                    quad_sum = quad if i == 0 else quad_sum + quad
+                if fresh:
+                    acc[group, 0, slot, re_rows, :] = co_sum
+                    acc[group, 1, slot, re_rows, :] = quad_sum
+                else:
+                    acc[group, 0, slot, re_rows, :] += co_sum
+                    acc[group, 1, slot, re_rows, :] += quad_sum
+            return carry
+
+        lax.fori_loop(0, half // step_rows, part, 0)
+
+    def relay(block):
+        to_far(block).wait_recv()
+        forward(block).start()
+
+    def finish(block):
+        to_mate(block).wait_recv()
+        forward(block).wait_recv()
+        cross(block)
+
+    count = len(ORDER)
+    for step in range(count + 2):
+        if step < count:
+            meridional(ORDER[step])
+            to_far(ORDER[step]).start()
+            to_mate(ORDER[step]).start()
+        if 0 <= step - 1 < count:
+            relay(ORDER[step - 1])
+        if 0 <= step - 2 < count:
+            finish(ORDER[step - 2])
+
+    scale = 1.0 / 8
+    for slot, b in enumerate((level, mate, far, far_mate)):
+        for c in range(2):
+            pair = acc[0, c, slot].T * scale
+            single = acc[1, c, slot].T * scale
+            out_ref[c, 0, b] = pair[:wave]
+            out_ref[c, 1, b] = pair[wave : 2 * wave]
+            out_ref[c, 2, b] = single[:wave] + single[wave : 2 * wave]
+
+    for block in range(len(BLOCKS)):
+        for d in range(1, space_size):
+            to_peer(block, d).wait_send()
+        to_mate(block).wait_send()
+        to_far(block).wait_send()
+        forward(block).wait_send()
+
+
+def by_kernel(fc_long, fc_short):
+    lat, lev_local, sample_count, var_count, lon_size = fc_long.shape
+    space_size = lax.axis_size("space")
+    wave = MK // space_size
+    table = zonal_table(lon_size, MK).reshape(lon_size, 2, space_size, wave).transpose(2, 0, 1, 3)
+    tables = np.zeros((2, space_size, lon_size, 2, LANES), jnp.bfloat16)
+    tables[0, ..., :wave] = table
+    tables[1, ..., wave : 2 * wave] = table
+    tables = tables.reshape(2, space_size, lon_size, 2 * LANES)
+    merid = merid_table(lat * space_size, NL).reshape(space_size, lat, 2, NL)
+    cos, sin = merid[:, :, 0], merid[:, :, 1]
+    stacked = np.stack([np.stack([cos, sin], axis=1), np.stack([-sin, cos], axis=1)])
+    stacked = stacked.transpose(0, 4, 1, 2, 3).reshape(2 * NL, space_size * 2 * lat)
+    diff = (fc_long.astype(jnp.float32) - fc_short.astype(jnp.float32)).astype(jnp.bfloat16)
+    diff = diff[:, 0].transpose(2, 1, 0, 3).reshape(var_count * sample_count * lat, lon_size)
+    blocks = len(BLOCKS)
+    rows = 2 * lat
+    vmem = pl.BlockSpec(memory_space=pltpu.VMEM)
+    sems = pltpu.SemaphoreType.DMA
+    out = pl.pallas_call(
+        functools.partial(kernel, space_size, lat, wave),
+        out_shape=jax.ShapeDtypeStruct((2, var_count, 4, wave, NL), jnp.float32),
+        in_specs=[vmem] * 3,
+        out_specs=vmem,
+        scratch_shapes=[
+            pltpu.VMEM((space_size, rows, TILES * LANES), jnp.bfloat16),
+            pltpu.VMEM((space_size * rows, TILES * LANES), jnp.bfloat16),
+            pltpu.VMEM((4, 2 * NL, TILES * LANES), jnp.bfloat16),
+            pltpu.VMEM((space_size, rows, LANES), jnp.float32),
+            pltpu.VMEM((2, 2, 4, NL, LANES), jnp.float32),
+            sems((blocks, space_size)),
+            sems((blocks, space_size)),
+        ]
+        + [sems((blocks,))] * 7,
+        compiler_params=pltpu.CompilerParams(
+            collective_id=0, has_side_effects=True, vmem_limit_bytes=56 * 1024 * 1024
+        ),
+    )(diff, jnp.asarray(tables), jnp.asarray(stacked))
+    return out[:, :, None]
+
+
+def on_device(fc_long, fc_short):
+    lat, lev_local, sample_count, var_count, lon_size = fc_long.shape
+    space_size = lax.axis_size("space")
+    fits = (
+        lat % 8 == 0
+        and 2 * (MK // space_size) == LANES - 16
+        and (lev_local, sample_count, var_count) == (1, 8, 3)
+        and lax.axis_size("level") == 4
+        and 2 * NL % 256 == 0
+    )
+    return by_kernel(fc_long, fc_short) if fits else by_collectives(fc_long, fc_short)
+
+
 def solution(mesh):
     placed = (P("space", "level", None, None, None), P("space", "level", None, None, None))
     return jax.shard_map(

time: 157 us -> 140 us (0.89); the launches traced: 155 us -> 140 us
  Pallas kernels: 0 us -> 120 us
  waiting for transfers between devices: 50.7 us -> 0 us
  matrix products: 33.9 us -> 0 us
  starting transfers between devices: 27.9 us -> 0 us
  local copies, waits for them, and re-layouts: 25.9 us -> 10.7 us
  other arithmetic: 15.8 us -> 9.18 us
    pallas_call x0 -> x1, Pallas kernels: none -> 120 us  [by_kernel(): pl.pallas_call(functools.partial(kernel, space_size, lat, wave), out_shap...]
    all_to_all x3 -> x0, waiting for transfers between devices: 39.5 us -> none  [on_device(): lax.all_to_all(coeff, 'space', split_axis=0, concat_axis=0, tiled=True)]
    dot_general x6 -> x0, matrix products: 33.9 us -> none  [the longest x3 25.2 us: on_device(): jnp.einsum('ysx,xpuk->pysuk', diff, zonal_tab, preferred_element_type=jnp...]
    all_to_all x3 -> x0, starting transfers between devices: 18.4 us -> none  [on_device(): lax.all_to_all(coeff, 'space', split_axis=0, concat_axis=0, tiled=True)]
    convert_element_type x3 -> x0, local copies, waits for them, and re-layouts: 13.3 us -> none  [on_device(): coeff = jnp.einsum('ysx,xpuk->pysuk', diff, zonal_tab, preferred_element_...]
    ppermute x9 -> x0, waiting for transfers between devices: 11.2 us -> none  [the longest x3 11.2 us: from_chip(): lax.ppermute(block, 'level', [((i + 2 * distance) % level_size, i) for i...]
    convert_element_type x12 -> x0, other arithmetic: 11 us -> none  [the longest x9 7.52 us: cross_pair(): other = other_spec.astype(jnp.float32)]
    ppermute x9 -> x0, starting transfers between devices: 9.57 us -> none  [the longest x6 6.89 us: swap_core(): return lax.ppermute(block, 'level', [(i, i ^ 1) for i in range(level_size)])]
  transfers between devices with their start and end apart: 12 -> 0, of which waited for: 5 -> 0; matrix products, arithmetic and copies ran while one was open for 37% -> 0% of each run, Pallas kernels for 0% -> 0%
where the time goes in v2:
time: 140 us
  Pallas kernels  120 us (86%)
  local copies, waits for them, and re-layouts  10.7 us (8%)
  other arithmetic  9.18 us (7%)
    pallas_call x1, Pallas kernels, by_kernel(): pl.pallas_call(functools.partial(kernel, space_size, lat, wave), out_shap...  120 us
    transpose x1, other arithmetic, by_kernel(): diff[:, 0].transpose(2, 1, 0, 3)  9.18 us
    transpose x1, local copies, waits for them, and re-layouts, by_kernel(): diff[:, 0].transpose(2, 1, 0, 3)  7.72 us
    unnamed x1, local copies, waits for them, and re-layouts  3.02 us

profile of v2, /device:TPU:13, one launch (start us, length us, event | category | flops | bytes accessed | tf_op | source)
XLA Modules:
  0.0 140.1 jit_solution(17356986988637077320)
XLA Ops:
  0.0 9.2 %fusion = bf16[3,8,88,1440]{3,1,0,2:T(8,128)(2,1)} fusion(bf16[88,1,8,3,1440]{4,2,3,1,0:T(8,128)(2,1)} %param.5, bf16[88,1,8,3,1440]{4,2,3,1,0:T(8,128)(2,1)} %param.4), kind=kLoop, calls=%fused_computation.1 | loop fusion | flops 12165120 | bytes 18247680 | tf_op jit(solution)/shard_map/transpose | solution.py:323
  9.2 7.7 %copy.5 = bf16[3,8,88,1440]{3,2,1,0:T(8,128)(2,1)} copy(bf16[3,8,88,1440]{3,1,0,2:T(8,128)(2,1)} %fusion) | data formatting | bytes 12165120 | tf_op jit(solution)/shard_map/transpose | solution.py:323
  16.9 120.1 %shard_map.46 = f32[2,3,4,56,384]{4,3,2,1,0:T(8,128)} custom-call(bf16[2112,1440]{1,0:T(8,128)(2,1)} %bitcast.8, bf16[2,8,1440,256]{3,2,1,0:T(8,128)(2,1)} %constant.4.clone.tab_ref, bf16[768,1408]{1,0:T(8,128)(2,1)} %constant.5.clone.merid_ref), custom_call_target="tpu_custom_call" | custom-call | tf_op jit(solution)/shard_map/pallas_call | solution.py:328
  137.1 3.0 %copy.8 = f32[2,3,1,4,56,384]{5,4,3,2,1,0:T(8,128)} copy(f32[2,3,1,4,56,384]{5,4,3,2,1,0:T(8,128)} %bitcast.9) | data formatting | bytes 4128768

commit v3 on v2

--- a/solution.py
+++ b/solution.py
@@ -93,21 +93,16 @@
 
 LANES = 128
 MESH = pl.DeviceIdType.MESH
-BLOCKS = (
-    ((0, 6), (1, 6), 6, 1, 0),
-    ((0, 0), (1, 0), 0, 2, 0),
-    ((0, 2), (1, 2), 2, 2, 0),
-    ((0, 4), (1, 4), 4, 2, 0),
-    ((2, 0), (2, 4), 7, 2, 1),
-    ((2, 2), (2, 6), 9, 2, 1),
-)
-ORDER = (1, 2, 3, 4, 5, 0)
+BLOCKS = ((7, 2, 1), (9, 2, 1), (0, 2, 0), (2, 2, 0), (4, 2, 0), (6, 1, 0))
 TILES = 11
+SAMPLES = 8
+IN_FLIGHT = 2
 
 
 def kernel(
-    space_size, lat, wave, diff_ref, tab_ref, merid_ref, out_ref,
-    send, recv, spec, last, acc,
+    space_size, lat, wave, long_hbm, short_hbm, tab_hbm, merid_hbm, out_ref,
+    long_in, short_in, tab, merid, diff, zbuf, send, recv, spec, acc,
+    in_sem, tab_sem, merid_sem,
     a2a_send, a2a_recv, own_sem, mate_send, mate_recv, far_send, far_recv, fwd_send, fwd_recv,
 ):
     me = lax.axis_index("space")
@@ -117,7 +112,24 @@
     far_mate = lax.rem(mate + 2, 4)
     rows = 2 * lat
     half = NL
+    pairs = space_size // 2
+    block_count = len(BLOCKS)
     own_rows = pl.ds(pl.multiple_of(me * rows, 16), rows)
+
+    def load(var):
+        return (
+            pltpu.make_async_copy(long_hbm.at[:, var], long_in.at[var], in_sem.at[0, var]),
+            pltpu.make_async_copy(short_hbm.at[:, var], short_in.at[var], in_sem.at[1, var]),
+        )
+
+    load_tab = pltpu.make_async_copy(tab_hbm, tab, tab_sem)
+    load_merid = pltpu.make_async_copy(merid_hbm, merid, merid_sem)
+    for copy in load(2):
+        copy.start()
+    load_tab.start()
+    for copy in load(0) + load(1):
+        copy.start()
+    load_merid.start()
 
     barrier = pltpu.get_barrier_semaphore()
     for d in range(1, space_size):
@@ -127,7 +139,7 @@
         pl.semaphore_signal(barrier, inc=1, device_id={"level": peer}, device_id_type=MESH)
 
     def columns(block):
-        first, count = BLOCKS[block][2:4]
+        first, count, _ = BLOCKS[block]
         return pl.ds(first * LANES, count * LANES)
 
     def to_peer(block, d):
@@ -168,72 +180,103 @@
     def forward(block):
         return to_level(block, mate, 2, 3, fwd_send, fwd_recv)
 
-    def zonal(block, d):
-        (var0, s0), (var1, s1), first, count, group = BLOCKS[block]
-        peer = lax.rem(me + d, space_size)
-        samples = 8
-        start0 = (var0 * samples + s0) * lat
-        start1 = (var1 * samples + s1) * lat
-        z = jnp.dot(
-            diff_ref[start0 : start0 + rows, :], tab_ref[0, peer],
-            preferred_element_type=jnp.float32,
-        ) + jnp.dot(
-            diff_ref[start1 : start1 + rows, :], tab_ref[1, peer],
-            preferred_element_type=jnp.float32,
-        )
+    def difference(var):
+        for copy in load(var):
+            copy.wait()
+
+        def part(r, carry):
+            lats = pl.ds(r * 8, 8)
+            delta = long_in[var, lats].astype(jnp.float32) - short_in[var, lats].astype(jnp.float32)
+            delta = delta.reshape(8 * SAMPLES, delta.shape[-1]).astype(jnp.bfloat16)
+            diff[var, pl.ds(pl.multiple_of(r * 8 * SAMPLES, 8 * SAMPLES), 8 * SAMPLES), :] = delta
+            return carry
+
+        lax.fori_loop(0, lat // 8, part, 0)
+
+    def zonal(var, slot, pair):
+        def part(r, carry):
+            some = pl.ds(pl.multiple_of(r * rows, 16), rows)
+            z = jnp.dot(diff[var, some, :], tab[pair], preferred_element_type=jnp.float32)
+            zbuf[slot, 0, some, :] = z[:, :LANES]
+            zbuf[slot, 1, some, :] = z[:, LANES:]
+            return carry
+
+        lax.fori_loop(0, SAMPLES // 2, part, 0)
+
+    def merged(slot0, s0, slot1, s1, j):
+        lane = lax.broadcasted_iota(jnp.int32, (lat, LANES), 1)
+        one = zbuf[slot0, j, pl.ds(s0, lat, stride=SAMPLES), :]
+        two = zbuf[slot1, j, pl.ds(s1, lat, stride=SAMPLES), :]
+        real = jnp.where(lane < wave, one, pltpu.roll(two, wave, 1))
+        imag = jnp.where(lane < wave, pltpu.roll(one, LANES - wave, 1), two)
+        return jnp.concatenate([real, imag], axis=0)
+
+    def put(peer, t, tile):
+        send[peer, :, t * LANES : (t + 1) * LANES] = tile.astype(jnp.bfloat16)
+
+    def single_tiles(i, carry):
+        pair = lax.rem(me // 2 + 1 + i, pairs)
+        zonal(2, 0, pair)
+        for j in range(2):
+            peer = 2 * pair + j
+            for t in range(4):
+                put(peer, 7 + t, merged(0, t, 0, t + 4, j))
+            d = lax.rem(peer - me + space_size, space_size)
+
+            @pl.when(peer != me)
+            def _():
+                for block in range(IN_FLIGHT):
+                    to_peer(block, d).start()
+
+        return carry
+
+    def pair_tiles(i, carry):
+        pair = lax.rem(me // 2 + 1 + i, pairs)
+        zonal(0, 0, pair)
+        zonal(1, 1, pair)
         lane = lax.broadcasted_iota(jnp.int32, (rows, LANES), 1)
-        tiles = [
-            jnp.concatenate([z[i * lat : (i + 1) * lat, :LANES], z[i * lat : (i + 1) * lat, LANES:]], axis=0)
-            for i in range(2)
-        ]
-        if count == 1:
-            last[peer] = tiles[1]
-        for i in range(count):
-            tile = tiles[i]
-            if group == 0:
-                t = first + i
-                extra = pltpu.roll(last[peer], 2 * wave - 16 * t, 1)
-                tile = jnp.where(lane < 2 * wave, tile, extra)
-            send[peer, :, (first + i) * LANES : (first + i + 1) * LANES] = tile.astype(jnp.bfloat16)
-
-    for block in range(len(BLOCKS)):
-        def one_peer(step, carry, block=block):
-            d = step + 1
-
-            @pl.when(d < space_size)
-            def _():
-                zonal(block, d)
-                if block > 0:
-                    to_peer(block, d).start()
-
-            return carry
-
-        if block == 1:
-            pl.semaphore_wait(barrier, space_size + 1)
-        lax.fori_loop(0, space_size - 1, one_peer, 0)
-        zonal(block, 0)
+        for j in range(2):
+            peer = 2 * pair + j
+            last = merged(0, 7, 1, 7, j)
+            for t in range(7):
+                extra = pltpu.roll(last, 2 * wave - 16 * t, 1)
+                put(peer, t, jnp.where(lane < 2 * wave, merged(0, t, 1, t, j), extra))
+        return carry
+
+    difference(2)
+    load_tab.wait()
+    pl.semaphore_wait(barrier, space_size + 1)
+    lax.fori_loop(0, pairs, single_tiles, 0)
+    difference(0)
+    difference(1)
+    lax.fori_loop(0, pairs, pair_tiles, 0)
+    for block in range(block_count):
         to_self(block).start()
-    for d in range(1, space_size):
-        to_peer(0, d).start()
+    load_merid.wait()
 
     def meridional(block):
-        first, count = BLOCKS[block][2:4]
+        first, count, _ = BLOCKS[block]
         cols = slice(first * LANES, (first + count) * LANES)
         for d in range(1, space_size):
             to_peer(block, d).wait_recv()
+            to_peer(block, d).wait_send()
+            if block + IN_FLIGHT < block_count:
+                to_peer(block + IN_FLIGHT, d).start()
         to_self(block).wait()
 
         def part(r, carry):
             r_rows = pl.ds(pl.multiple_of(r * 256, 256), 256)
-            total = jnp.dot(merid_ref[r_rows, :], recv[:, cols], preferred_element_type=jnp.float32)
+            total = jnp.dot(merid[r_rows, :], recv[:, cols], preferred_element_type=jnp.float32)
             spec[0, r_rows, cols] = total.astype(jnp.bfloat16)
             return carry
 
         lax.fori_loop(0, 2 * half // 256, part, 0)
-
-    def cross(block):
-        first, count, group = BLOCKS[block][2:]
-        fresh = block in (1, 4)
+        to_far(block).start()
+        to_mate(block).start()
+
+    def cross(block, slots):
+        first, count, group = BLOCKS[block]
+        fresh = block == [g for _, _, g in BLOCKS].index(group)
         step_rows = 32
 
         def part(r, carry):
@@ -241,8 +284,8 @@
             re_rows = pl.ds(base, step_rows)
             im_rows = pl.ds(pl.multiple_of(half + r * step_rows, step_rows), step_rows)
             lane = lax.broadcasted_iota(jnp.int32, (step_rows, LANES), 1)
-            for slot in range(4):
-                co_sum = None
+            for slot in slots:
+                co_sum = quad_sum = None
                 for i in range(count):
                     t = first + i
                     cols = slice(t * LANES, (t + 1) * LANES)
@@ -258,7 +301,7 @@
                         co = co + jnp.where(here, pltpu.roll(co, shift, 1), 0.0)
                         quad = quad + jnp.where(here, pltpu.roll(quad, shift, 1), 0.0)
                     co_sum = co if co_sum is None else co_sum + co
-                    quad_sum = quad if i == 0 else quad_sum + quad
+                    quad_sum = quad if quad_sum is None else quad_sum + quad
                 if fresh:
                     acc[group, 0, slot, re_rows, :] = co_sum
                     acc[group, 1, slot, re_rows, :] = quad_sum
@@ -269,28 +312,9 @@
 
         lax.fori_loop(0, half // step_rows, part, 0)
 
-    def relay(block):
-        to_far(block).wait_recv()
-        forward(block).start()
-
-    def finish(block):
-        to_mate(block).wait_recv()
-        forward(block).wait_recv()
-        cross(block)
-
-    count = len(ORDER)
-    for step in range(count + 2):
-        if step < count:
-            meridional(ORDER[step])
-            to_far(ORDER[step]).start()
-            to_mate(ORDER[step]).start()
-        if 0 <= step - 1 < count:
-            relay(ORDER[step - 1])
-        if 0 <= step - 2 < count:
-            finish(ORDER[step - 2])
-
-    scale = 1.0 / 8
-    for slot, b in enumerate((level, mate, far, far_mate)):
+    scale = 1.0 / SAMPLES
+
+    def write(slot, b):
         for c in range(2):
             pair = acc[0, c, slot].T * scale
             single = acc[1, c, slot].T * scale
@@ -298,9 +322,36 @@
             out_ref[c, 1, b] = pair[wave : 2 * wave]
             out_ref[c, 2, b] = single[:wave] + single[wave : 2 * wave]
 
-    for block in range(len(BLOCKS)):
-        for d in range(1, space_size):
-            to_peer(block, d).wait_send()
+    def relay(block):
+        to_far(block).wait_recv()
+        forward(block).start()
+
+    def finish(block):
+        to_mate(block).wait_recv()
+        forward(block).wait_recv()
+        cross(block, range(4))
+
+    for block in range(block_count):
+        meridional(block)
+        if block >= 1:
+            relay(block - 1)
+        if block >= 2:
+            finish(block - 2)
+    final = block_count - 1
+    cross(final, (0,))
+    finish(final - 1)
+    write(0, level)
+    to_mate(final).wait_recv()
+    cross(final, (1,))
+    relay(final)
+    write(1, mate)
+    cross(final, (2,))
+    write(2, far)
+    forward(final).wait_recv()
+    cross(final, (3,))
+    write(3, far_mate)
+
+    for block in range(block_count):
         to_mate(block).wait_send()
         to_far(block).wait_send()
         forward(block).wait_send()
@@ -310,40 +361,51 @@
     lat, lev_local, sample_count, var_count, lon_size = fc_long.shape
     space_size = lax.axis_size("space")
     wave = MK // space_size
-    table = zonal_table(lon_size, MK).reshape(lon_size, 2, space_size, wave).transpose(2, 0, 1, 3)
-    tables = np.zeros((2, space_size, lon_size, 2, LANES), jnp.bfloat16)
-    tables[0, ..., :wave] = table
-    tables[1, ..., wave : 2 * wave] = table
-    tables = tables.reshape(2, space_size, lon_size, 2 * LANES)
+    pairs = space_size // 2
+    rows = 2 * lat
+    table = zonal_table(lon_size, MK).reshape(lon_size, 2, pairs, 2, wave).transpose(2, 0, 3, 1, 4)
+    padded = np.zeros((pairs, lon_size, 2, LANES), jnp.bfloat16)
+    padded[..., : 2 * wave] = table.reshape(pairs, lon_size, 2, 2 * wave)
+    padded = padded.reshape(pairs, lon_size, 2 * LANES)
     merid = merid_table(lat * space_size, NL).reshape(space_size, lat, 2, NL)
     cos, sin = merid[:, :, 0], merid[:, :, 1]
     stacked = np.stack([np.stack([cos, sin], axis=1), np.stack([-sin, cos], axis=1)])
-    stacked = stacked.transpose(0, 4, 1, 2, 3).reshape(2 * NL, space_size * 2 * lat)
-    diff = (fc_long.astype(jnp.float32) - fc_short.astype(jnp.float32)).astype(jnp.bfloat16)
-    diff = diff[:, 0].transpose(2, 1, 0, 3).reshape(var_count * sample_count * lat, lon_size)
+    stacked = stacked.transpose(0, 4, 1, 2, 3).reshape(2 * NL, space_size * rows)
     blocks = len(BLOCKS)
-    rows = 2 * lat
-    vmem = pl.BlockSpec(memory_space=pltpu.VMEM)
     sems = pltpu.SemaphoreType.DMA
+    bf16 = jnp.bfloat16
     out = pl.pallas_call(
         functools.partial(kernel, space_size, lat, wave),
         out_shape=jax.ShapeDtypeStruct((2, var_count, 4, wave, NL), jnp.float32),
-        in_specs=[vmem] * 3,
-        out_specs=vmem,
+        in_specs=[pl.BlockSpec(memory_space=pl.ANY)] * 4,
+        out_specs=pl.BlockSpec(memory_space=pltpu.VMEM),
         scratch_shapes=[
-            pltpu.VMEM((space_size, rows, TILES * LANES), jnp.bfloat16),
-            pltpu.VMEM((space_size * rows, TILES * LANES), jnp.bfloat16),
-            pltpu.VMEM((4, 2 * NL, TILES * LANES), jnp.bfloat16),
-            pltpu.VMEM((space_size, rows, LANES), jnp.float32),
+            pltpu.VMEM((var_count, lat, sample_count, lon_size), bf16),
+            pltpu.VMEM((var_count, lat, sample_count, lon_size), bf16),
+            pltpu.VMEM(padded.shape, bf16),
+            pltpu.VMEM(stacked.shape, bf16),
+            pltpu.VMEM((var_count, lat * sample_count, lon_size), bf16),
+            pltpu.VMEM((2, 2, lat * sample_count, LANES), jnp.float32),
+            pltpu.VMEM((space_size, rows, TILES * LANES), bf16),
+            pltpu.VMEM((space_size * rows, TILES * LANES), bf16),
+            pltpu.VMEM((4, 2 * NL, TILES * LANES), bf16),
             pltpu.VMEM((2, 2, 4, NL, LANES), jnp.float32),
+            sems((2, var_count)),
+            sems,
+            sems,
             sems((blocks, space_size)),
             sems((blocks, space_size)),
         ]
         + [sems((blocks,))] * 7,
         compiler_params=pltpu.CompilerParams(
-            collective_id=0, has_side_effects=True, vmem_limit_bytes=56 * 1024 * 1024
+            collective_id=0, has_side_effects=True, vmem_limit_bytes=58 * 1024 * 1024
         ),
-    )(diff, jnp.asarray(tables), jnp.asarray(stacked))
+    )(
+        fc_long[:, 0].transpose(0, 2, 1, 3),
+        fc_short[:, 0].transpose(0, 2, 1, 3),
+        jnp.asarray(padded),
+        jnp.asarray(stacked),
+    )
     return out[:, :, None]
 
 
@@ -353,7 +415,8 @@
     fits = (
         lat % 8 == 0
         and 2 * (MK // space_size) == LANES - 16
-        and (lev_local, sample_count, var_count) == (1, 8, 3)
+        and (lev_local, sample_count, var_count) == (1, SAMPLES, 3)
+        and space_size % 2 == 0
         and lax.axis_size("level") == 4
         and 2 * NL % 256 == 0
     )

time: 140 us -> 118 us (0.84)
  other arithmetic: 9.18 us -> 0 us
  local copies, waits for them, and re-layouts: 10.7 us -> 3.02 us
  Pallas kernels: 120 us -> 115 us
    transpose x1 -> x0, other arithmetic: 9.18 us -> none  [by_kernel(): diff[:, 0].transpose(2, 1, 0, 3)]
    transpose x1 -> x0, local copies, waits for them, and re-layouts: 7.72 us -> none  [by_kernel(): diff[:, 0].transpose(2, 1, 0, 3)]
    pallas_call x1, Pallas kernels: 120 us -> 115 us  [by_kernel(): pl.pallas_call(functools.partial(kernel, space_size, lat, wave), out_shap...]
where the time goes in v3:
time: 118 us
  Pallas kernels  115 us (97%)
  local copies, waits for them, and re-layouts  3.02 us (3%)
    pallas_call x1, Pallas kernels, by_kernel(): pl.pallas_call(functools.partial(kernel, space_size, lat, wave), out_shap...  115 us
    unnamed x1, local copies, waits for them, and re-layouts  3.02 us

profile of v3, /device:TPU:13, one launch (start us, length us, event | category | flops | bytes accessed | tf_op | source)
XLA Modules:
  0.0 117.9 jit_solution(7360483265299880738)
XLA Ops:
  0.0 114.9 %shard_map.46 = f32[2,3,4,56,384]{4,3,2,1,0:T(8,128)} custom-call(bf16[88,3,8,1440]{3,2,1,0:T(8,128)(2,1)} %bitcast.10, bf16[88,3,8,1440]{3,2,1,0:T(8,128)(2,1)} %bitcast.11, bf16[4,1440,256]{2,1,0:T(8,128)(2,1)} %constant.4.clone.tab_hbm, bf16[768,1408]{1,0:T(8,128)(2,1)} %constant.5.clone.merid_hbm), custom_call_target="tpu_custom_call" | custom-call | tf_op jit(solution)/shard_map/pallas_call | solution.py:377
  114.9 3.0 %copy.7 = f32[2,3,1,4,56,384]{5,4,3,2,1,0:T(8,128)} copy(f32[2,3,1,4,56,384]{5,4,3,2,1,0:T(8,128)} %bitcast.9) | data formatting | bytes 4128768

commit v4 on v3

--- a/solution.py
+++ b/solution.py
@@ -93,15 +93,17 @@
 
 LANES = 128
 MESH = pl.DeviceIdType.MESH
-BLOCKS = ((7, 2, 1), (9, 2, 1), (0, 2, 0), (2, 2, 0), (4, 2, 0), (6, 1, 0))
-TILES = 11
+BLOCKS = ((7, 3, 1), (0, 2, 0), (2, 2, 0), (4, 2, 0), (6, 1, 0))
+HALF = len(BLOCKS)
+TILES = 10
 SAMPLES = 8
 IN_FLIGHT = 2
 
 
 def kernel(
-    space_size, lat, wave, long_hbm, short_hbm, tab_hbm, merid_hbm, out_ref,
-    long_in, short_in, tab, merid, diff, zbuf, send, recv, spec, acc,
+    space_size, lat, wave, long_hbm, short_hbm, tab_hbm, merid_hbm, merid_half_hbm, out_ref,
+    long_in, short_in, tab, merid, merid_half, diff, zbuf,
+    send, recv, spec, send_half, recv_half, spec_half, acc,
     in_sem, tab_sem, merid_sem,
     a2a_send, a2a_recv, own_sem, mate_send, mate_recv, far_send, far_recv, fwd_send, fwd_recv,
 ):
@@ -113,7 +115,8 @@
     rows = 2 * lat
     half = NL
     pairs = space_size // 2
-    block_count = len(BLOCKS)
+    padded = recv_half.shape[0] // space_size
+    own_half = pl.ds(pl.multiple_of(me * padded, 16), padded)
     own_rows = pl.ds(pl.multiple_of(me * rows, 16), rows)
 
     def load(var):
@@ -123,13 +126,11 @@
         )
 
     load_tab = pltpu.make_async_copy(tab_hbm, tab, tab_sem)
-    load_merid = pltpu.make_async_copy(merid_hbm, merid, merid_sem)
+    load_merid = pltpu.make_async_copy(merid_hbm, merid, merid_sem.at[0])
+    load_half = pltpu.make_async_copy(merid_half_hbm, merid_half, merid_sem.at[1])
     for copy in load(2):
         copy.start()
     load_tab.start()
-    for copy in load(0) + load(1):
-        copy.start()
-    load_merid.start()
 
     barrier = pltpu.get_barrier_semaphore()
     for d in range(1, space_size):
@@ -144,10 +145,14 @@
 
     def to_peer(block, d):
         peer = lax.rem(me + d, space_size)
-        cols = columns(block)
+        if block == HALF:
+            source, target = send_half.at[peer], recv_half.at[own_half]
+        else:
+            cols = columns(block)
+            source, target = send.at[peer, :, cols], recv.at[own_rows, cols]
         return pltpu.make_async_remote_copy(
-            src_ref=send.at[peer, :, cols],
-            dst_ref=recv.at[own_rows, cols],
+            src_ref=source,
+            dst_ref=target,
             send_sem=a2a_send.at[block, d],
             recv_sem=a2a_recv.at[block, d],
             device_id={"space": peer},
@@ -155,16 +160,24 @@
         )
 
     def to_self(block):
+        if block == HALF:
+            return pltpu.make_async_copy(
+                send_half.at[me], recv_half.at[own_half], own_sem.at[block]
+            )
         cols = columns(block)
         return pltpu.make_async_copy(
             send.at[me, :, cols], recv.at[own_rows, cols], own_sem.at[block]
         )
 
     def to_level(block, peer, source, slot, send_sem, recv_sem):
-        cols = columns(block)
+        if block == HALF:
+            first, second = spec_half.at[source], spec_half.at[slot]
+        else:
+            cols = columns(block)
+            first, second = spec.at[source, :, cols], spec.at[slot, :, cols]
         return pltpu.make_async_remote_copy(
-            src_ref=spec.at[source, :, cols],
-            dst_ref=spec.at[slot, :, cols],
+            src_ref=first,
+            dst_ref=second,
             send_sem=send_sem.at[block],
             recv_sem=recv_sem.at[block],
             device_id={"level": peer},
@@ -181,9 +194,6 @@
         return to_level(block, mate, 2, 3, fwd_send, fwd_recv)
 
     def difference(var):
-        for copy in load(var):
-            copy.wait()
-
         def part(r, carry):
             lats = pl.ds(r * 8, 8)
             delta = long_in[var, lats].astype(jnp.float32) - short_in[var, lats].astype(jnp.float32)
@@ -211,58 +221,86 @@
         imag = jnp.where(lane < wave, pltpu.roll(one, LANES - wave, 1), two)
         return jnp.concatenate([real, imag], axis=0)
 
-    def put(peer, t, tile):
+    def put(peer, t, tile, spread, part):
+        lane = lax.broadcasted_iota(jnp.int32, (rows, LANES), 1)
+        extra = pltpu.roll(spread, 2 * wave - 16 * part, 1)
+        tile = jnp.where(lane < 2 * wave, tile, extra)
         send[peer, :, t * LANES : (t + 1) * LANES] = tile.astype(jnp.bfloat16)
+
+    def start_peer(block, peer):
+        d = lax.rem(peer - me + space_size, space_size)
+
+        @pl.when(peer != me)
+        def _():
+            to_peer(block, d).start()
 
     def single_tiles(i, carry):
         pair = lax.rem(me // 2 + 1 + i, pairs)
         zonal(2, 0, pair)
+        lane = lax.broadcasted_iota(jnp.int32, (lat, LANES), 1)
         for j in range(2):
             peer = 2 * pair + j
-            for t in range(4):
-                put(peer, 7 + t, merged(0, t, 0, t + 4, j))
-            d = lax.rem(peer - me + space_size, space_size)
-
-            @pl.when(peer != me)
-            def _():
-                for block in range(IN_FLIGHT):
-                    to_peer(block, d).start()
-
+            spread = merged(0, 3, 0, 7, j)
+            for t in range(3):
+                put(peer, 7 + t, merged(0, t, 0, t + 4, j), spread, t)
+            start_peer(0, peer)
+            rest = jnp.where(
+                lane < 64,
+                pltpu.roll(spread[:lat], LANES - 48, 1),
+                pltpu.roll(spread[lat:], 64 - 48, 1),
+            )
+            rest = jnp.concatenate([rest, jnp.zeros((padded - lat, LANES), jnp.float32)], axis=0)
+            send_half[peer] = rest.astype(jnp.bfloat16)
         return carry
 
     def pair_tiles(i, carry):
         pair = lax.rem(me // 2 + 1 + i, pairs)
         zonal(0, 0, pair)
         zonal(1, 1, pair)
-        lane = lax.broadcasted_iota(jnp.int32, (rows, LANES), 1)
         for j in range(2):
             peer = 2 * pair + j
-            last = merged(0, 7, 1, 7, j)
+            spread = merged(0, 7, 1, 7, j)
             for t in range(7):
-                extra = pltpu.roll(last, 2 * wave - 16 * t, 1)
-                put(peer, t, jnp.where(lane < 2 * wave, merged(0, t, 1, t, j), extra))
+                put(peer, t, merged(0, t, 1, t, j), spread, t)
+            start_peer(1, peer)
         return carry
 
+    for copy in load(2):
+        copy.wait()
+    load_tab.wait()
+    for copy in load(0) + load(1):
+        copy.start()
+    load_merid.start()
+    load_half.start()
     difference(2)
-    load_tab.wait()
     pl.semaphore_wait(barrier, space_size + 1)
     lax.fori_loop(0, pairs, single_tiles, 0)
-    difference(0)
-    difference(1)
+    for var in (0, 1):
+        for copy in load(var):
+            copy.wait()
+        difference(var)
     lax.fori_loop(0, pairs, pair_tiles, 0)
-    for block in range(block_count):
+    for block in range(HALF + 1):
         to_self(block).start()
     load_merid.wait()
+    load_half.wait()
+
+    def arrive(block):
+        for d in range(1, space_size):
+            to_peer(block, d).wait_recv()
+            to_peer(block, d).wait_send()
+            if block + IN_FLIGHT <= HALF:
+                to_peer(block + IN_FLIGHT, d).start()
+        to_self(block).wait()
+
+    def share(block):
+        to_far(block).start()
+        to_mate(block).start()
 
     def meridional(block):
         first, count, _ = BLOCKS[block]
         cols = slice(first * LANES, (first + count) * LANES)
-        for d in range(1, space_size):
-            to_peer(block, d).wait_recv()
-            to_peer(block, d).wait_send()
-            if block + IN_FLIGHT < block_count:
-                to_peer(block + IN_FLIGHT, d).start()
-        to_self(block).wait()
+        arrive(block)
 
         def part(r, carry):
             r_rows = pl.ds(pl.multiple_of(r * 256, 256), 256)
@@ -271,10 +309,37 @@
             return carry
 
         lax.fori_loop(0, 2 * half // 256, part, 0)
-        to_far(block).start()
-        to_mate(block).start()
-
-    def cross(block, slots):
+        share(block)
+
+    def meridional_half():
+        arrive(HALF)
+        lane = lax.broadcasted_iota(jnp.int32, (half, LANES), 1)
+        total = jnp.dot(merid_half[...], recv_half[...], preferred_element_type=jnp.float32)
+        turned = pltpu.roll(total[half:], 64, 1)
+        both = total[:half] + jnp.where(lane < 64, turned, -turned)
+        spec_half[0] = both.astype(jnp.bfloat16)
+        share(HALF)
+
+    def cross_half(slot):
+        step_rows = 64
+
+        def part(r, carry):
+            some = pl.ds(pl.multiple_of(r * step_rows, step_rows), step_rows)
+            lane = lax.broadcasted_iota(jnp.int32, (step_rows, LANES), 1)
+            here = (lane >= 48) & (lane < 48 + 64)
+            a = spec_half[0, some, :].astype(jnp.float32)
+            b = spec_half[slot, some, :].astype(jnp.float32)
+            same = a * b
+            mixed = a * pltpu.roll(b, 64, 1)
+            co = same + pltpu.roll(same, 64, 1)
+            quad = pltpu.roll(mixed, 64, 1) - mixed
+            acc[1, 0, slot, some, :] += jnp.where(here, pltpu.roll(co, 48, 1), 0.0)
+            acc[1, 1, slot, some, :] += jnp.where(here, pltpu.roll(quad, 48, 1), 0.0)
+            return carry
+
+        lax.fori_loop(0, half // step_rows, part, 0)
+
+    def cross(block):
         first, count, group = BLOCKS[block]
         fresh = block == [g for _, _, g in BLOCKS].index(group)
         step_rows = 32
@@ -284,7 +349,7 @@
             re_rows = pl.ds(base, step_rows)
             im_rows = pl.ds(pl.multiple_of(half + r * step_rows, step_rows), step_rows)
             lane = lax.broadcasted_iota(jnp.int32, (step_rows, LANES), 1)
-            for slot in slots:
+            for slot in range(4):
                 co_sum = quad_sum = None
                 for i in range(count):
                     t = first + i
@@ -295,11 +360,10 @@
                     b_im = spec[slot, im_rows, cols].astype(jnp.float32)
                     co = a_re * b_re + a_im * b_im
                     quad = a_im * b_re - a_re * b_im
-                    if group == 0:
-                        here = (lane >= 16 * t) & (lane < 16 * t + 16)
-                        shift = (16 * t + 16) % LANES
-                        co = co + jnp.where(here, pltpu.roll(co, shift, 1), 0.0)
-                        quad = quad + jnp.where(here, pltpu.roll(quad, shift, 1), 0.0)
+                    low = 16 * (t - 7 * group)
+                    here = (lane >= low) & (lane < low + 16)
+                    co = co + jnp.where(here, pltpu.roll(co, low + 16, 1), 0.0)
+                    quad = quad + jnp.where(here, pltpu.roll(quad, low + 16, 1), 0.0)
                     co_sum = co if co_sum is None else co_sum + co
                     quad_sum = quad if quad_sum is None else quad_sum + quad
                 if fresh:
@@ -329,29 +393,30 @@
     def finish(block):
         to_mate(block).wait_recv()
         forward(block).wait_recv()
-        cross(block, range(4))
-
-    for block in range(block_count):
+        cross(block)
+
+    for block in range(HALF):
         meridional(block)
-        if block >= 1:
-            relay(block - 1)
-        if block >= 2:
-            finish(block - 2)
-    final = block_count - 1
-    cross(final, (0,))
-    finish(final - 1)
+        if block == HALF - 1:
+            finish(block - 1)
+        relay(block)
+        if block < HALF - 2:
+            finish(block)
+    meridional_half()
+    finish(HALF - 1)
+    cross_half(0)
     write(0, level)
-    to_mate(final).wait_recv()
-    cross(final, (1,))
-    relay(final)
+    to_mate(HALF).wait_recv()
+    cross_half(1)
+    relay(HALF)
     write(1, mate)
-    cross(final, (2,))
+    cross_half(2)
     write(2, far)
-    forward(final).wait_recv()
-    cross(final, (3,))
+    forward(HALF).wait_recv()
+    cross_half(3)
     write(3, far_mate)
 
-    for block in range(block_count):
+    for block in range(HALF + 1):
         to_mate(block).wait_send()
         to_far(block).wait_send()
         forward(block).wait_send()
@@ -363,6 +428,7 @@
     wave = MK // space_size
     pairs = space_size // 2
     rows = 2 * lat
+    bf16 = jnp.bfloat16
     table = zonal_table(lon_size, MK).reshape(lon_size, 2, pairs, 2, wave).transpose(2, 0, 3, 1, 4)
     padded = np.zeros((pairs, lon_size, 2, LANES), jnp.bfloat16)
     padded[..., : 2 * wave] = table.reshape(pairs, lon_size, 2, 2 * wave)
@@ -371,28 +437,35 @@
     cos, sin = merid[:, :, 0], merid[:, :, 1]
     stacked = np.stack([np.stack([cos, sin], axis=1), np.stack([-sin, cos], axis=1)])
     stacked = stacked.transpose(0, 4, 1, 2, 3).reshape(2 * NL, space_size * rows)
-    blocks = len(BLOCKS)
+    row_pad = -(-lat // 16) * 16
+    halves = np.zeros((2, NL, space_size, row_pad), bf16)
+    halves[..., :lat] = np.stack([cos, sin]).transpose(0, 3, 1, 2)
+    halves = halves.reshape(2 * NL, space_size * row_pad)
+    blocks = HALF + 1
     sems = pltpu.SemaphoreType.DMA
-    bf16 = jnp.bfloat16
     out = pl.pallas_call(
         functools.partial(kernel, space_size, lat, wave),
         out_shape=jax.ShapeDtypeStruct((2, var_count, 4, wave, NL), jnp.float32),
-        in_specs=[pl.BlockSpec(memory_space=pl.ANY)] * 4,
+        in_specs=[pl.BlockSpec(memory_space=pl.ANY)] * 5,
         out_specs=pl.BlockSpec(memory_space=pltpu.VMEM),
         scratch_shapes=[
             pltpu.VMEM((var_count, lat, sample_count, lon_size), bf16),
             pltpu.VMEM((var_count, lat, sample_count, lon_size), bf16),
             pltpu.VMEM(padded.shape, bf16),
             pltpu.VMEM(stacked.shape, bf16),
+            pltpu.VMEM(halves.shape, bf16),
             pltpu.VMEM((var_count, lat * sample_count, lon_size), bf16),
             pltpu.VMEM((2, 2, lat * sample_count, LANES), jnp.float32),
             pltpu.VMEM((space_size, rows, TILES * LANES), bf16),
             pltpu.VMEM((space_size * rows, TILES * LANES), bf16),
             pltpu.VMEM((4, 2 * NL, TILES * LANES), bf16),
+            pltpu.VMEM((space_size, row_pad, LANES), bf16),
+            pltpu.VMEM((space_size * row_pad, LANES), bf16),
+            pltpu.VMEM((4, NL, LANES), bf16),
             pltpu.VMEM((2, 2, 4, NL, LANES), jnp.float32),
             sems((2, var_count)),
             sems,
-            sems,
+            sems((2,)),
             sems((blocks, space_size)),
             sems((blocks, space_size)),
         ]
@@ -405,6 +478,7 @@
         fc_short[:, 0].transpose(0, 2, 1, 3),
         jnp.asarray(padded),
         jnp.asarray(stacked),
+        jnp.asarray(halves),
     )
     return out[:, :, None]
 

time: 118 us -> 131 us (1.11)
  Pallas kernels: 115 us -> 128 us
    pallas_call x1, Pallas kernels: 115 us -> 128 us  [by_kernel(): pl.pallas_call(functools.partial(kernel, space_size, lat, wave), out_shap...]
where the time goes in v4:
time: 131 us
  Pallas kernels  128 us (98%)
  local copies, waits for them, and re-layouts  3.02 us (2%)
    pallas_call x1, Pallas kernels, by_kernel(): pl.pallas_call(functools.partial(kernel, space_size, lat, wave), out_shap...  128 us
    unnamed x1, local copies, waits for them, and re-layouts  3.02 us

profile of v4, /device:TPU:13, one launch (start us, length us, event | category | flops | bytes accessed | tf_op | source)
XLA Modules:
  0.0 130.9 jit_solution(6448264593096226336)
XLA Ops:
  0.0 127.8 %shard_map.55 = f32[2,3,4,56,384]{4,3,2,1,0:T(8,128)} custom-call(bf16[88,3,8,1440]{3,2,1,0:T(8,128)(2,1)} %bitcast.10, bf16[88,3,8,1440]{3,2,1,0:T(8,128)(2,1)} %bitcast.11, bf16[4,1440,256]{2,1,0:T(8,128)(2,1)} %constant.6.clone.tab_hbm, bf16[768,1408]{1,0:T(8,128)(2,1)} %constant.7.clone.merid_hbm, bf16[768,768]{1,0:T(8,128)(2,1)} %constant.8.clone.merid_half_hbm), custom_call_target="tpu_custom_call" | custom-call | tf_op jit(solution)/shard_map/pallas_call | solution.py:446
  127.9 3.0 %copy.8 = f32[2,3,1,4,56,384]{5,4,3,2,1,0:T(8,128)} copy(f32[2,3,1,4,56,384]{5,4,3,2,1,0:T(8,128)} %bitcast.9) | data formatting | bytes 4128768

commit v5 on v4

--- a/solution.py
+++ b/solution.py
@@ -97,7 +97,6 @@
 HALF = len(BLOCKS)
 TILES = 10
 SAMPLES = 8
-IN_FLIGHT = 2
 
 
 def kernel(
@@ -280,6 +279,9 @@
             copy.wait()
         difference(var)
     lax.fori_loop(0, pairs, pair_tiles, 0)
+    for block in range(2, HALF + 1):
+        for d in range(1, space_size):
+            to_peer(block, lax.rem(d + 1, space_size - 1) + 1).start()
     for block in range(HALF + 1):
         to_self(block).start()
     load_merid.wait()
@@ -288,9 +290,6 @@
     def arrive(block):
         for d in range(1, space_size):
             to_peer(block, d).wait_recv()
-            to_peer(block, d).wait_send()
-            if block + IN_FLIGHT <= HALF:
-                to_peer(block + IN_FLIGHT, d).start()
         to_self(block).wait()
 
     def share(block):
@@ -397,11 +396,12 @@
 
     for block in range(HALF):
         meridional(block)
-        if block == HALF - 1:
-            finish(block - 1)
-        relay(block)
-        if block < HALF - 2:
-            finish(block)
+        if block >= 1:
+            relay(block - 1)
+        if block >= 2:
+            finish(block - 2)
+    finish(HALF - 2)
+    relay(HALF - 1)
     meridional_half()
     finish(HALF - 1)
     cross_half(0)
@@ -417,6 +417,8 @@
     write(3, far_mate)
 
     for block in range(HALF + 1):
+        for d in range(1, space_size):
+            to_peer(block, d).wait_send()
         to_mate(block).wait_send()
         to_far(block).wait_send()
         forward(block).wait_send()

time: 131 us -> 116 us (0.89)
  Pallas kernels: 128 us -> 113 us
    pallas_call x1, Pallas kernels: 128 us -> 113 us  [by_kernel(): pl.pallas_call(functools.partial(kernel, space_size, lat, wave), out_shap...]
where the time goes in v5:
time: 116 us
  Pallas kernels  113 us (97%)
  local copies, waits for them, and re-layouts  3.02 us (3%)
    pallas_call x1, Pallas kernels, by_kernel(): pl.pallas_call(functools.partial(kernel, space_size, lat, wave), out_shap...  113 us
    unnamed x1, local copies, waits for them, and re-layouts  3.02 us

profile of v5, /device:TPU:13, one launch (start us, length us, event | category | flops | bytes accessed | tf_op | source)
XLA Modules:
  0.0 115.8 jit_solution(16237644411943291913)
XLA Ops:
  0.0 112.8 %shard_map.55 = f32[2,3,4,56,384]{4,3,2,1,0:T(8,128)} custom-call(bf16[88,3,8,1440]{3,2,1,0:T(8,128)(2,1)} %bitcast.10, bf16[88,3,8,1440]{3,2,1,0:T(8,128)(2,1)} %bitcast.11, bf16[4,1440,256]{2,1,0:T(8,128)(2,1)} %constant.6.clone.tab_hbm, bf16[768,1408]{1,0:T(8,128)(2,1)} %constant.7.clone.merid_hbm, bf16[768,768]{1,0:T(8,128)(2,1)} %constant.8.clone.merid_half_hbm), custom_call_target="tpu_custom_call" | custom-call | tf_op jit(solution)/shard_map/pallas_call | solution.py:448
  112.8 3.0 %copy.8 = f32[2,3,1,4,56,384]{5,4,3,2,1,0:T(8,128)} copy(f32[2,3,1,4,56,384]{5,4,3,2,1,0:T(8,128)} %bitcast.9) | data formatting | bytes 4128768

commit v6 on v5

--- a/solution.py
+++ b/solution.py
@@ -97,6 +97,7 @@
 HALF = len(BLOCKS)
 TILES = 10
 SAMPLES = 8
+IN_FLIGHT = 3
 
 
 def kernel(
@@ -233,8 +234,25 @@
         def _():
             to_peer(block, d).start()
 
+    def pair_at(i):
+        place = me // 2
+        middle = pairs // 2
+        upper = place // middle
+        depth = place + upper * (pairs - 1 - 2 * place)
+        order = lax.rem(i + middle * lax.rem(depth + 1, 2), pairs)
+        return order + upper * (pairs - 1 - 2 * order)
+
+    def start_block(block):
+        def one_pair(i, carry):
+            pair = pair_at(i)
+            for j in range(2):
+                start_peer(block, 2 * pair + j)
+            return carry
+
+        lax.fori_loop(0, pairs, one_pair, 0)
+
     def single_tiles(i, carry):
-        pair = lax.rem(me // 2 + 1 + i, pairs)
+        pair = pair_at(i)
         zonal(2, 0, pair)
         lane = lax.broadcasted_iota(jnp.int32, (lat, LANES), 1)
         for j in range(2):
@@ -253,7 +271,7 @@
         return carry
 
     def pair_tiles(i, carry):
-        pair = lax.rem(me // 2 + 1 + i, pairs)
+        pair = pair_at(i)
         zonal(0, 0, pair)
         zonal(1, 1, pair)
         for j in range(2):
@@ -279,9 +297,8 @@
             copy.wait()
         difference(var)
     lax.fori_loop(0, pairs, pair_tiles, 0)
-    for block in range(2, HALF + 1):
-        for d in range(1, space_size):
-            to_peer(block, lax.rem(d + 1, space_size - 1) + 1).start()
+    for block in range(2, IN_FLIGHT):
+        start_block(block)
     for block in range(HALF + 1):
         to_self(block).start()
     load_merid.wait()
@@ -290,6 +307,8 @@
     def arrive(block):
         for d in range(1, space_size):
             to_peer(block, d).wait_recv()
+        if block + IN_FLIGHT <= HALF:
+            start_block(block + IN_FLIGHT)
         to_self(block).wait()
 
     def share(block):
@@ -492,7 +511,7 @@
         lat % 8 == 0
         and 2 * (MK // space_size) == LANES - 16
         and (lev_local, sample_count, var_count) == (1, SAMPLES, 3)
-        and space_size % 2 == 0
+        and space_size % 4 == 0
         and lax.axis_size("level") == 4
         and 2 * NL % 256 == 0
     )

time: 116 us -> 117 us (level)
  the two profiles are of different devices: /device:TPU:13 before, /device:TPU:5 now
where the time goes in v6:
time: 117 us
  Pallas kernels  114 us (97%)
  local copies, waits for them, and re-layouts  3.02 us (3%)
    pallas_call x1, Pallas kernels, by_kernel(): pl.pallas_call(functools.partial(kernel, space_size, lat, wave), out_shap...  114 us
    unnamed x1, local copies, waits for them, and re-layouts  3.02 us

profile of v6, /device:TPU:5, one launch (start us, length us, event | category | flops | bytes accessed | tf_op | source)
XLA Modules:
  0.0 117.2 jit_solution(11140237689208493407)
XLA Ops:
  0.0 114.2 %shard_map.55 = f32[2,3,4,56,384]{4,3,2,1,0:T(8,128)} custom-call(bf16[88,3,8,1440]{3,2,1,0:T(8,128)(2,1)} %bitcast.10, bf16[88,3,8,1440]{3,2,1,0:T(8,128)(2,1)} %bitcast.11, bf16[4,1440,256]{2,1,0:T(8,128)(2,1)} %constant.6.clone.tab_hbm, bf16[768,1408]{1,0:T(8,128)(2,1)} %constant.7.clone.merid_hbm, bf16[768,768]{1,0:T(8,128)(2,1)} %constant.8.clone.merid_half_hbm), custom_call_target="tpu_custom_call" | custom-call | tf_op jit(solution)/shard_map/pallas_call | solution.py:467
  114.2 3.0 %copy.8 = f32[2,3,1,4,56,384]{5,4,3,2,1,0:T(8,128)} copy(f32[2,3,1,4,56,384]{5,4,3,2,1,0:T(8,128)} %bitcast.9) | data formatting | bytes 4128768

commit v7 on v6

--- a/solution.py
+++ b/solution.py
@@ -204,14 +204,9 @@
         lax.fori_loop(0, lat // 8, part, 0)
 
     def zonal(var, slot, pair):
-        def part(r, carry):
-            some = pl.ds(pl.multiple_of(r * rows, 16), rows)
-            z = jnp.dot(diff[var, some, :], tab[pair], preferred_element_type=jnp.float32)
-            zbuf[slot, 0, some, :] = z[:, :LANES]
-            zbuf[slot, 1, some, :] = z[:, LANES:]
-            return carry
-
-        lax.fori_loop(0, SAMPLES // 2, part, 0)
+        z = jnp.dot(diff[var], tab[pair], preferred_element_type=jnp.float32)
+        zbuf[slot, 0] = z[:, :LANES]
+        zbuf[slot, 1] = z[:, LANES:]
 
     def merged(slot0, s0, slot1, s1, j):
         lane = lax.broadcasted_iota(jnp.int32, (lat, LANES), 1)
@@ -280,6 +275,7 @@
             for t in range(7):
                 put(peer, t, merged(0, t, 1, t, j), spread, t)
             start_peer(1, peer)
+            start_peer(2, peer)
         return carry
 
     for copy in load(2):
@@ -296,19 +292,13 @@
         for copy in load(var):
             copy.wait()
         difference(var)
-    lax.fori_loop(0, pairs, pair_tiles, 0)
-    for block in range(2, IN_FLIGHT):
-        start_block(block)
-    for block in range(HALF + 1):
-        to_self(block).start()
-    load_merid.wait()
-    load_half.wait()
 
     def arrive(block):
         for d in range(1, space_size):
             to_peer(block, d).wait_recv()
-        if block + IN_FLIGHT <= HALF:
+        if block > 0 and block + IN_FLIGHT <= HALF:
             start_block(block + IN_FLIGHT)
+        to_self(block).start()
         to_self(block).wait()
 
     def share(block):
@@ -413,10 +403,15 @@
         forward(block).wait_recv()
         cross(block)
 
-    for block in range(HALF):
+    lax.fori_loop(0, pairs // 2, pair_tiles, 0)
+    load_merid.wait()
+    load_half.wait()
+    meridional(0)
+    lax.fori_loop(pairs // 2, pairs, pair_tiles, 0)
+    start_block(IN_FLIGHT)
+    for block in range(1, HALF):
         meridional(block)
-        if block >= 1:
-            relay(block - 1)
+        relay(block - 1)
         if block >= 2:
             finish(block - 2)
     finish(HALF - 2)

time: 117 us -> 118 us (level)
  no operation moved by 1% of the time
where the time goes in v7:
time: 118 us; the launch traced here: 117 us
  Pallas kernels  114 us (97%)
  local copies, waits for them, and re-layouts  3.02 us (3%)
    pallas_call x1, Pallas kernels, by_kernel(): pl.pallas_call(functools.partial(kernel, space_size, lat, wave), out_shap...  114 us
    unnamed x1, local copies, waits for them, and re-layouts  3.02 us

profile of v7, /device:TPU:5, one launch (start us, length us, event | category | flops | bytes accessed | tf_op | source)
XLA Modules:
  0.0 117.4 jit_solution(1334652859035837054)
XLA Ops:
  0.0 114.4 %shard_map.55 = f32[2,3,4,56,384]{4,3,2,1,0:T(8,128)} custom-call(bf16[88,3,8,1440]{3,2,1,0:T(8,128)(2,1)} %bitcast.10, bf16[88,3,8,1440]{3,2,1,0:T(8,128)(2,1)} %bitcast.11, bf16[4,1440,256]{2,1,0:T(8,128)(2,1)} %constant.6.clone.tab_hbm, bf16[768,1408]{1,0:T(8,128)(2,1)} %constant.7.clone.merid_hbm, bf16[768,768]{1,0:T(8,128)(2,1)} %constant.8.clone.merid_half_hbm), custom_call_target="tpu_custom_call" | custom-call | tf_op jit(solution)/shard_map/pallas_call | solution.py:462
  114.4 3.0 %copy.8 = f32[2,3,1,4,56,384]{5,4,3,2,1,0:T(8,128)} copy(f32[2,3,1,4,56,384]{5,4,3,2,1,0:T(8,128)} %bitcast.9) | data formatting | bytes 4128768

commit v8 on v7

--- a/solution.py
+++ b/solution.py
@@ -95,7 +95,6 @@
 MESH = pl.DeviceIdType.MESH
 BLOCKS = ((7, 3, 1), (0, 2, 0), (2, 2, 0), (4, 2, 0), (6, 1, 0))
 HALF = len(BLOCKS)
-TILES = 10
 SAMPLES = 8
 IN_FLIGHT = 3
 
@@ -139,17 +138,12 @@
     for peer in (mate, far):
         pl.semaphore_signal(barrier, inc=1, device_id={"level": peer}, device_id_type=MESH)
 
-    def columns(block):
-        first, count, _ = BLOCKS[block]
-        return pl.ds(first * LANES, count * LANES)
-
     def to_peer(block, d):
         peer = lax.rem(me + d, space_size)
         if block == HALF:
             source, target = send_half.at[peer], recv_half.at[own_half]
         else:
-            cols = columns(block)
-            source, target = send.at[peer, :, cols], recv.at[own_rows, cols]
+            source, target = send[block].at[peer], recv[block].at[own_rows]
         return pltpu.make_async_remote_copy(
             src_ref=source,
             dst_ref=target,
@@ -164,17 +158,15 @@
             return pltpu.make_async_copy(
                 send_half.at[me], recv_half.at[own_half], own_sem.at[block]
             )
-        cols = columns(block)
         return pltpu.make_async_copy(
-            send.at[me, :, cols], recv.at[own_rows, cols], own_sem.at[block]
+            send[block].at[me], recv[block].at[own_rows], own_sem.at[block]
         )
 
     def to_level(block, peer, source, slot, send_sem, recv_sem):
         if block == HALF:
             first, second = spec_half.at[source], spec_half.at[slot]
         else:
-            cols = columns(block)
-            first, second = spec.at[source, :, cols], spec.at[slot, :, cols]
+            first, second = spec[block].at[source], spec[block].at[slot]
         return pltpu.make_async_remote_copy(
             src_ref=first,
             dst_ref=second,
@@ -220,7 +212,10 @@
         lane = lax.broadcasted_iota(jnp.int32, (rows, LANES), 1)
         extra = pltpu.roll(spread, 2 * wave - 16 * part, 1)
         tile = jnp.where(lane < 2 * wave, tile, extra)
-        send[peer, :, t * LANES : (t + 1) * LANES] = tile.astype(jnp.bfloat16)
+        for block, (first, count, _) in enumerate(BLOCKS):
+            if first <= t < first + count:
+                cols = slice((t - first) * LANES, (t - first + 1) * LANES)
+                send[block][peer, :, cols] = tile.astype(jnp.bfloat16)
 
     def start_peer(block, peer):
         d = lax.rem(peer - me + space_size, space_size)
@@ -306,14 +301,12 @@
         to_mate(block).start()
 
     def meridional(block):
-        first, count, _ = BLOCKS[block]
-        cols = slice(first * LANES, (first + count) * LANES)
         arrive(block)
 
         def part(r, carry):
             r_rows = pl.ds(pl.multiple_of(r * 256, 256), 256)
-            total = jnp.dot(merid[r_rows, :], recv[:, cols], preferred_element_type=jnp.float32)
-            spec[0, r_rows, cols] = total.astype(jnp.bfloat16)
+            total = jnp.dot(merid[r_rows, :], recv[block][...], preferred_element_type=jnp.float32)
+            spec[block][0, r_rows, :] = total.astype(jnp.bfloat16)
             return carry
 
         lax.fori_loop(0, 2 * half // 256, part, 0)
@@ -361,11 +354,11 @@
                 co_sum = quad_sum = None
                 for i in range(count):
                     t = first + i
-                    cols = slice(t * LANES, (t + 1) * LANES)
-                    a_re = spec[0, re_rows, cols].astype(jnp.float32)
-                    a_im = spec[0, im_rows, cols].astype(jnp.float32)
-                    b_re = spec[slot, re_rows, cols].astype(jnp.float32)
-                    b_im = spec[slot, im_rows, cols].astype(jnp.float32)
+                    cols = slice(i * LANES, (i + 1) * LANES)
+                    a_re = spec[block][0, re_rows, cols].astype(jnp.float32)
+                    a_im = spec[block][0, im_rows, cols].astype(jnp.float32)
+                    b_re = spec[block][slot, re_rows, cols].astype(jnp.float32)
+                    b_im = spec[block][slot, im_rows, cols].astype(jnp.float32)
                     co = a_re * b_re + a_im * b_im
                     quad = a_im * b_re - a_re * b_im
                     low = 16 * (t - 7 * group)
@@ -458,6 +451,7 @@
     halves[..., :lat] = np.stack([cos, sin]).transpose(0, 3, 1, 2)
     halves = halves.reshape(2 * NL, space_size * row_pad)
     blocks = HALF + 1
+    widths = [count * LANES for _, count, _ in BLOCKS]
     sems = pltpu.SemaphoreType.DMA
     out = pl.pallas_call(
         functools.partial(kernel, space_size, lat, wave),
@@ -472,9 +466,9 @@
             pltpu.VMEM(halves.shape, bf16),
             pltpu.VMEM((var_count, lat * sample_count, lon_size), bf16),
             pltpu.VMEM((2, 2, lat * sample_count, LANES), jnp.float32),
-            pltpu.VMEM((space_size, rows, TILES * LANES), bf16),
-            pltpu.VMEM((space_size * rows, TILES * LANES), bf16),
-            pltpu.VMEM((4, 2 * NL, TILES * LANES), bf16),
+            [pltpu.VMEM((space_size, rows, width), bf16) for width in widths],
+            [pltpu.VMEM((space_size * rows, width), bf16) for width in widths],
+            [pltpu.VMEM((4, 2 * NL, width), bf16) for width in widths],
             pltpu.VMEM((space_size, row_pad, LANES), bf16),
             pltpu.VMEM((space_size * row_pad, LANES), bf16),
             pltpu.VMEM((4, NL, LANES), bf16),

time: 118 us -> 118 us (level)
  no operation moved by 1% of the time
where the time goes in v8:
time: 118 us
  Pallas kernels  114 us (97%)
  local copies, waits for them, and re-layouts  3.02 us (3%)
    pallas_call x1, Pallas kernels, by_kernel(): pl.pallas_call(functools.partial(kernel, space_size, lat, wave), out_shap...  114 us
    unnamed x1, local copies, waits for them, and re-layouts  3.02 us

profile of v8, /device:TPU:5, one launch (start us, length us, event | category | flops | bytes accessed | tf_op | source)
XLA Modules:
  0.0 117.5 jit_solution(5140532233981492250)
XLA Ops:
  0.0 114.5 %shard_map.55 = f32[2,3,4,56,384]{4,3,2,1,0:T(8,128)} custom-call(bf16[88,3,8,1440]{3,2,1,0:T(8,128)(2,1)} %bitcast.10, bf16[88,3,8,1440]{3,2,1,0:T(8,128)(2,1)} %bitcast.11, bf16[4,1440,256]{2,1,0:T(8,128)(2,1)} %constant.6.clone.tab_hbm, bf16[768,1408]{1,0:T(8,128)(2,1)} %constant.7.clone.merid_hbm, bf16[768,768]{1,0:T(8,128)(2,1)} %constant.8.clone.merid_half_hbm), custom_call_target="tpu_custom_call" | custom-call | tf_op jit(solution)/shard_map/pallas_call | solution.py:456
  114.5 3.0 %copy.8 = f32[2,3,1,4,56,384]{5,4,3,2,1,0:T(8,128)} copy(f32[2,3,1,4,56,384]{5,4,3,2,1,0:T(8,128)} %bitcast.9) | data formatting | bytes 4128768
